TPU v7x, 128 devices: a whole 4x4x4 slice. The times are simulated.
128 devices in a mesh: pipe: 2 (over core), tensor: 4 (over z), dp: 16 (over y, x).
Axes of the slice: x: 4, y: 4, z: 4, core: 2. Of those that a mesh axis runs over, the one named last changes fastest.
Arguments:
- tokens: bfloat16 [16384, 1024], P('dp'), may hold values from -6 to 6
- cotangent: bfloat16 [16384, 1024], P('dp'), may hold values from -6 to 6
- segment_ids: int32 [16, 1024], P('dp'), may hold values from 0 to 3, never falling along the last dimension, each value on 1 to 512 neighbouring positions
- mixer_gain: float32 [2, 1024], P('pipe', 'dp'), may hold values from 0.1 to 1.9
- ffn_gain: float32 [2, 1024], P('pipe', 'dp'), may hold values from 0.1 to 1.9
- gate_master: float32 [2, 1024, 4608], P('pipe', 'dp', 'tensor'), may hold values from -0.1875 to 0.1875
- up_master: float32 [2, 1024, 4608], P('pipe', 'dp', 'tensor'), may hold values from -0.1875 to 0.1875
- down_master: float32 [2, 4608, 1024], P('pipe', 'tensor', 'dp'), may hold values from -0.09375 to 0.09375
- conv_in: float32 [1024, 3, 1024], P(('pipe', 'dp'), None, 'tensor'), may hold values from -0.1875 to 0.1875
- conv_kernel: float32 [3, 1024], P(None, 'tensor'), may hold values from -3.5 to 3.5
- conv_out: float32 [1024, 1024], P('tensor', ('pipe', 'dp')), may hold values from -0.1875 to 0.1875
- query_master: float32 [1024, 1024], P(('pipe', 'dp'), 'tensor'), may hold values from -0.1875 to 0.1875
- key_master: float32 [1024, 512], P(('pipe', 'dp'), 'tensor'), may hold values from -0.1875 to 0.1875
- value_master: float32 [1024, 512], P(('pipe', 'dp'), 'tensor'), may hold values from -0.1875 to 0.1875
- query_gain: float32 [64], replicated, may hold values from 0.1 to 1.9
- key_gain: float32 [64], replicated, may hold values from 0.1 to 1.9
- output_master: float32 [1024, 1024], P('tensor', ('pipe', 'dp')), may hold values from -1.5 to 1.5
Outputs:
- section_outputs: bfloat16 [2, 16384, 1024], P('pipe', 'dp')
- input_grads: float32 [2, 16384, 1024], P('pipe', 'dp')
- grad_mixer_gain: float32 [2, 1024], P('pipe', 'dp')
- grad_ffn_gain: float32 [2, 1024], P('pipe', 'dp')
- grad_gate: float32 [2, 1024, 4608], P('pipe', 'dp', 'tensor')
- grad_up: float32 [2, 1024, 4608], P('pipe', 'dp', 'tensor')
- grad_down: float32 [2, 4608, 1024], P('pipe', 'tensor', 'dp')
- grad_conv_in: float32 [1024, 3, 1024], P(('pipe', 'dp'), None, 'tensor')
- grad_conv_kernel: float32 [3, 1024], replicated
- grad_conv_out: float32 [1024, 1024], P('tensor', ('pipe', 'dp'))
- grad_query: float32 [1024, 1024], P(('pipe', 'dp'), 'tensor')
- grad_key: float32 [1024, 512], P(('pipe', 'dp'), 'tensor')
- grad_value: float32 [1024, 512], P(('pipe', 'dp'), 'tensor')
- grad_query_gain: float32 [64], replicated
- grad_key_gain: float32 [64], replicated
- grad_output: float32 [1024, 1024], P('tensor', ('pipe', 'dp'))
Inputs may be any that keep to these rules, and one draw needn't show every extreme that they name: `segment_ids`: along each sequence the document numbers never fall; equal numbers mark one document.
All inputs are finite; a program needn't handle non-finite values.
Results may differ from a plain program's by a relative error of at most 0.025.
The roundings to bfloat16 on the way count: a program that leaves them out, or rounds other values in their place, can miss the bound.
Values may be sent and summed in bfloat16 or wider, within the bound.
No kernel may reach another device: no remote copies, remote signals or barrier semaphores. Data moves between devices by JAX's collectives and lax.ppermute only.
A program may use at most 384 MiB of HBM per device.

v0:
```python
import functools

import jax
import jax.numpy as jnp
from jax import lax
from jax.experimental import pallas as pl
from jax.experimental.pallas import tpu as pltpu
from jax.sharding import Mesh
from jax.sharding import PartitionSpec as P

DP = ("dp_0", "dp_1")
PIPE_DP = ("pipe", "dp_0", "dp_1")
EPS = 1e-05
THETA = 1000000.0
NEGATIVE = -1e30
HALO = 16
BF = jnp.bfloat16
F32 = jnp.float32


def dot(left, right, dims=((1,), (0,))):
    return lax.dot_general(left, right, (dims, ((), ())), preferred_element_type=F32)


def dot_cols(left, right):
    return dot(left, right, ((1,), (1,)))


def dot_rows(left, right):
    return dot(left, right, ((0,), (0,)))


def exchange(parts, axis):
    return lax.all_to_all(parts, axis, 0, 0)


def scatter_sum(value, axis):
    size = lax.axis_size(axis)
    parts = value.reshape(size, value.shape[0] // size, *value.shape[1:])
    return jnp.sum(exchange(parts, axis).astype(F32), axis=0)


def gather(value, axis):
    size = lax.axis_size(axis)
    parts = exchange(jnp.broadcast_to(value[None], (size, *value.shape)), axis)
    return parts.reshape(size * value.shape[0], *value.shape[1:])


def turned(value, axis, by):
    size = lax.axis_size(axis)
    return lax.ppermute(value, axis, [(i, (i + by) % size) for i in range(size)])


def direct_scatter_sum(value, axis):
    me = lax.axis_index(axis)
    rows = value.shape[0] // 4

    def block(by):
        return lax.dynamic_slice_in_dim(value, lax.rem(me + by, 4) * rows, rows, 0)

    total = block(0).astype(F32)
    for by in (1, 3, 2):
        total = total + turned(block(by), axis, by).astype(F32)
    return total


def direct_gather(value, axis):
    me = lax.axis_index(axis)
    whole = jnp.zeros((4, *value.shape), value.dtype)
    for by in (0, 1, 3, 2):
        part = turned(value, axis, by) if by else value
        whole = lax.dynamic_update_slice_in_dim(whole, part[None], lax.rem(me + 4 - by, 4), 0)
    return whole.reshape(4 * value.shape[0], *value.shape[1:])


def after(value, *others):
    return lax.optimization_barrier((value, *others))[0]


def other_core(value):
    return lax.ppermute(value, "pipe", [(0, 1), (1, 0)])


def in_core_order(core, own, other):
    return jnp.where(
        core == 0, jnp.concatenate([own, other], 0), jnp.concatenate([other, own], 0)
    )


def half_of(value, core):
    rows = value.shape[0] // 2
    return lax.dynamic_slice_in_dim(value, core * rows, rows, 0)


def rms_forward(value, gain):
    scale = lax.rsqrt(jnp.mean(value * value, axis=-1, keepdims=True) + EPS)
    return value * scale * gain, scale


def rms_backward(value, scale, gain, grad):
    weighted = grad * gain
    inner = jnp.mean(weighted * value, axis=-1, keepdims=True)
    return scale * weighted - value * (scale * scale * scale) * inner


def positions_of(segments):
    first = jnp.sum((segments[None, :] < segments[:, None]).astype(jnp.int32), axis=1)
    return jnp.arange(segments.shape[0], dtype=jnp.int32) - first


def rotation(positions, head_dim):
    half = head_dim // 2
    frequency = THETA ** (-2.0 * jnp.arange(half, dtype=F32) / head_dim)
    angle = positions.astype(F32)[:, None] * frequency[None, :]
    cosine, sine = jnp.cos(angle), jnp.sin(angle)
    return jnp.tile(cosine, (1, 4)), jnp.tile(jnp.concatenate([-sine, sine], 1), (1, 2))


def whole(kernel, out_shapes, *operands, scratch=(), flops=0, vmem=40):
    spec = pl.BlockSpec(memory_space=pltpu.VMEM)
    moved = sum(x.size * x.dtype.itemsize for x in (*operands, *out_shapes))
    return pl.pallas_call(
        kernel,
        out_shape=tuple(out_shapes),
        in_specs=[spec] * len(operands),
        out_specs=tuple(spec for _ in out_shapes),
        scratch_shapes=scratch,
        compiler_params=pltpu.CompilerParams(vmem_limit_bytes=vmem * 2**20),
        cost_estimate=pl.CostEstimate(flops=flops, bytes_accessed=moved, transcendentals=0),
    )(*operands)


def head_mean(value, low):
    first = jnp.sum(jnp.where(low, value, 0.0), axis=1, keepdims=True)
    second = jnp.sum(jnp.where(low, 0.0, value), axis=1, keepdims=True)
    return jnp.where(low, first, second) * (1.0 / 64.0)


def partner(value, first_half):
    return jnp.where(first_half, pltpu.roll(value, 96, 1), pltpu.roll(value, 32, 1))


def lanes_of(rows):
    lane = lax.broadcasted_iota(jnp.int32, (rows, 128), 1)
    return lane < 64, (lane & 63) < 32


CHUNK = 128


def rope_forward_kernel(raw_ref, cosine_ref, sine_ref, gain_ref, out_ref):
    rows = raw_ref.shape[0]
    low, first_half = lanes_of(CHUNK)

    @pl.loop(0, rows // CHUNK)
    def _(step):
        at = pl.ds(pl.multiple_of(step * CHUNK, CHUNK), CHUNK)
        cosine, sine = cosine_ref[at, :], sine_ref[at, :]
        for tile in range(3):
            cols = pl.ds(tile * 128, 128)
            value = raw_ref[at, cols]
            gain = gain_ref[pl.ds(tile // 2, 1), :]
            normed = value * lax.rsqrt(head_mean(value * value, low) + EPS) * gain
            turned = normed * cosine + partner(normed, first_half) * sine
            out_ref[at, cols] = turned.astype(BF)
        out_ref[at, pl.ds(384, 128)] = raw_ref[at, pl.ds(384, 128)].astype(BF)


def rope_backward_kernel(
    raw_ref, grad_query_ref, grad_kv_ref, more_kv_ref, cosine_ref, sine_ref, gain_ref, out_ref, sums_ref
):
    rows = raw_ref.shape[0]
    low, first_half = lanes_of(CHUNK)
    sums_ref[...] = jnp.zeros_like(sums_ref)

    @pl.loop(0, rows // CHUNK)
    def _(step):
        at = pl.ds(pl.multiple_of(step * CHUNK, CHUNK), CHUNK)
        cosine, sine = cosine_ref[at, :], sine_ref[at, :]
        for tile in range(3):
            cols = pl.ds(tile * 128, 128)
            if tile < 2:
                grad = grad_query_ref[at, cols]
            else:
                grad = grad_kv_ref[at, pl.ds(0, 128)] + more_kv_ref[at, pl.ds(0, 128)]
            grad = grad * cosine - partner(grad, first_half) * sine
            value = raw_ref[at, cols]
            gain = gain_ref[pl.ds(tile // 2, 1), :]
            scale = lax.rsqrt(head_mean(value * value, low) + EPS)
            weighted = grad * gain
            inner = head_mean(weighted * value, low)
            back = scale * weighted - value * (scale * scale * scale) * inner
            out_ref[at, cols] = back.astype(BF)
            sums_ref[pl.ds(tile // 2, 1), :] += jnp.sum(grad * value * scale, axis=0, keepdims=True)
        out_ref[at, pl.ds(384, 128)] = (
            grad_kv_ref[at, pl.ds(128, 128)] + more_kv_ref[at, pl.ds(128, 128)]
        ).astype(BF)


def fill_window(own_ref, before_ref, keys_ref):
    rows = own_ref.shape[0]
    keys_ref[pl.ds(0, rows), :] = before_ref[...]
    keys_ref[pl.ds(rows, rows), :] = own_ref[:, pl.ds(256, 256)]


def bias_of(column_ref, row_ref, start, block, span):
    keys = column_ref[pl.ds(start, span), pl.ds(0, 1)]
    queries = row_ref[pl.ds(0, 1), pl.ds(start, block)]
    key_at = lax.broadcasted_iota(jnp.int32, (span, block), 0)
    query_at = lax.broadcasted_iota(jnp.int32, (span, block), 1) + (span - block)
    return jnp.where((key_at <= query_at) & (keys == queries), 0.0, NEGATIVE)


BLOCK = 256
SPAN = 768


def attend_forward_kernel(own_ref, before_ref, column_ref, row_ref, out_ref, log_ref, keys_ref):
    rows = own_ref.shape[0]
    fill_window(own_ref, before_ref, keys_ref)
    log_ref[...] = jnp.zeros_like(log_ref)
    for sub in range(rows // BLOCK):
        start = sub * BLOCK
        bias = bias_of(column_ref, row_ref, start, BLOCK, SPAN)
        values = keys_ref[pl.ds(start, SPAN), pl.ds(128, 128)].astype(F32).T.astype(BF)
        parts = []
        for head in range(4):
            kv = head // 2
            key = keys_ref[pl.ds(start, SPAN), pl.ds(kv * 64, 64)]
            query = own_ref[pl.ds(start, BLOCK), pl.ds(head * 64, 64)] * jnp.asarray(0.125, BF)
            scores = dot_cols(key, query) + bias
            top = jnp.max(scores, axis=0, keepdims=True)
            weights = jnp.exp(scores - top)
            total = jnp.sum(weights, axis=0, keepdims=True)
            probs = (weights * (1.0 / total)).astype(BF)
            parts.append(dot(values[kv * 64 : kv * 64 + 64], probs))
            log_ref[pl.ds(head, 1), pl.ds(start, BLOCK)] = top + jnp.log(total)
        out_ref[pl.ds(start, BLOCK), :] = jnp.concatenate(parts, 0).T.astype(BF)


def attend_backward_kernel(
    own_ref, before_ref, column_ref, row_ref, log_ref, grad_ref, query_ref, kv_ref, keys_ref
):
    rows = own_ref.shape[0]
    fill_window(own_ref, before_ref, keys_ref)
    kv_ref[...] = jnp.zeros_like(kv_ref)
    for sub in range(rows // BLOCK):
        start = sub * BLOCK
        window = pl.ds(start, SPAN)
        bias = bias_of(column_ref, row_ref, start, BLOCK, SPAN)
        keys = keys_ref[window, pl.ds(0, 128)].astype(F32).T.astype(BF)
        parts = []
        for kv in range(2):
            key = keys_ref[window, pl.ds(kv * 64, 64)]
            value = keys_ref[window, pl.ds(128 + kv * 64, 64)]
            grad_key = jnp.zeros((SPAN, 64), F32)
            grad_value = jnp.zeros((SPAN, 64), F32)
            for head in (2 * kv, 2 * kv + 1):
                query = own_ref[pl.ds(start, BLOCK), pl.ds(head * 64, 64)] * jnp.asarray(0.125, BF)
                grad = grad_ref[pl.ds(start, BLOCK), pl.ds(head * 64, 64)]
                log = log_ref[pl.ds(head, 1), pl.ds(start, BLOCK)]
                probs = jnp.exp(dot_cols(key, query) + bias - log)
                grad_probs = dot_cols(value, grad)
                shared = jnp.sum(probs * grad_probs, axis=0, keepdims=True)
                grad_scores = (probs * (grad_probs - shared)).astype(BF)
                grad_key += dot(grad_scores, query)
                grad_value += dot(probs.astype(BF), grad)
                parts.append(dot(keys[kv * 64 : kv * 64 + 64], grad_scores) * 0.125)
            kv_ref[window, pl.ds(kv * 64, 64)] += grad_key
            kv_ref[window, pl.ds(128 + kv * 64, 64)] += grad_value
        query_ref[pl.ds(start, BLOCK), :] = jnp.concatenate(parts, 0).T


HALF = 32
GATE, UP, DOWN = range(3)


def fetch_weights(core_ref, own_ref, other_ref, weights_ref, sems, order):
    core = core_ref[0]

    def copies(k):
        return [
            pltpu.make_async_copy(
                ref.at[:, pl.ds(HALF * k, HALF), :], weights_ref.at[k, :, part], sems.at[k, side]
            )
            for side, (ref, part) in enumerate(((own_ref, core), (other_ref, 1 - core)))
        ]

    for k in order:
        for copy in copies(k):
            copy.start()

    def matrix(k):
        for copy in copies(k):
            copy.wait()
        return lambda: weights_ref[k].reshape(-1, weights_ref.shape[-1])

    return matrix


def gates_back(grad_inner, gate, up):
    sigma = 1.0 / (1.0 + jnp.exp(-gate))
    silu = gate * sigma
    grad_gate = grad_inner * up * (sigma * (1.0 + gate * (1.0 - sigma)))
    return grad_gate.astype(BF), (grad_inner * silu).astype(BF), (silu * up).astype(BF)


def silu(gate):
    return gate * (1.0 / (1.0 + jnp.exp(-gate)))


class Moved:
    def __init__(self, source, target, sem):
        self.copy = pltpu.make_async_copy(source, target, sem)

    def start(self):
        self.copy.start()
        return self

    def wait(self):
        self.copy.wait()


def feed_forward_kernel(
    core_ref, in_ref, own_ref, other_ref, acts_ref, out_ref, held_ref, weights_ref, sems, out_sems
):
    matrix = fetch_weights(core_ref, own_ref, other_ref, weights_ref, sems, (GATE, UP, DOWN))
    held_ref[0] = dot(in_ref[...], matrix(GATE)())
    first = Moved(held_ref.at[0], acts_ref.at[0], out_sems.at[0]).start()
    held_ref[1] = dot(in_ref[...], matrix(UP)())
    second = Moved(held_ref.at[1], acts_ref.at[1], out_sems.at[1]).start()
    inner = (silu(held_ref[0]) * held_ref[1]).astype(BF)
    out_ref[...] = dot_cols(inner, matrix(DOWN)()).astype(BF)
    first.wait()
    second.wait()


def send_parts(parts_ref, held_ref, sems):
    return [Moved(held_ref.at[k], parts_ref.at[k], sems.at[k]).start() for k in range(3)]


def feed_backward_kernel(
    core_ref, grad_ref, own_ref, other_ref, acts_ref, parts_ref, out_ref,
    acts_held_ref, held_ref, weights_ref, sems, in_sems, out_sems,
):
    matrix = fetch_weights(core_ref, own_ref, other_ref, weights_ref, sems, (DOWN,))
    acts = [Moved(acts_ref.at[k], acts_held_ref.at[k], in_sems.at[k]).start() for k in range(2)]
    more = fetch_weights(core_ref, own_ref, other_ref, weights_ref, sems, (GATE, UP))
    grad_inner = dot(grad_ref[...], matrix(DOWN)())
    acts[0].wait()
    acts[1].wait()
    grad_gate, grad_up, inner = gates_back(grad_inner, acts_held_ref[0], acts_held_ref[1])
    held_ref[0] = grad_gate
    held_ref[1] = grad_up
    held_ref[2] = inner
    sent = send_parts(parts_ref, held_ref, out_sems)
    out = dot_cols(held_ref[0], more(GATE)())
    out_ref[...] = (out + dot_cols(held_ref[1], more(UP)())).astype(BF)
    for copy in sent:
        copy.wait()


def feed_both_kernel(
    core_ref, in_ref, grad_ref, own_ref, other_ref, parts_ref, second_ref, out_ref,
    held_ref, weights_ref, sems, out_sems,
):
    matrix = fetch_weights(core_ref, own_ref, other_ref, weights_ref, sems, (DOWN, GATE, UP))
    down = matrix(DOWN)
    grad_inner = dot(grad_ref[...], down())
    gate_w = matrix(GATE)
    gate = dot(in_ref[...], gate_w())
    up_w = matrix(UP)
    up = dot(in_ref[...], up_w())
    grad_gate, grad_up, inner = gates_back(grad_inner, gate, up)
    held_ref[0] = grad_gate
    held_ref[1] = grad_up
    held_ref[2] = inner
    sent = send_parts(parts_ref, held_ref, out_sems)
    out = dot_cols(held_ref[0], gate_w())
    out_ref[...] = (out + dot_cols(held_ref[1], up_w())).astype(BF)
    second_ref[...] = dot_cols(held_ref[2], down()).astype(BF)
    for copy in sent:
        copy.wait()


def feed_weights_kernel(
    core_ref, in_ref, grad_ref, part_ref, keep_ref, send_ref, in_t_ref, grad_t_ref, both_ref
):
    core = core_ref[0]
    step = pl.program_id(0)

    @pl.when(step == 0)
    def _():
        in_t_ref[...] = in_ref[...].astype(F32).T.astype(BF)
        grad_t_ref[...] = grad_ref[...].astype(F32).T.astype(BF)

    @pl.when(step < 2)
    def _():
        both_ref[...] = dot(in_t_ref[...], part_ref[0]).astype(BF).reshape(both_ref.shape)

    @pl.when(step == 2)
    def _():
        both_ref[...] = dot(grad_t_ref[...], part_ref[0]).astype(BF).reshape(both_ref.shape)

    keep_ref[...] = both_ref[:, core]
    send_ref[...] = both_ref[:, 1 - core]


SMEM_SPEC = pl.BlockSpec(memory_space=pltpu.SMEM)
HBM_SPEC = pl.BlockSpec(memory_space=pltpu.HBM)
VMEM_SPEC = pl.BlockSpec(memory_space=pltpu.VMEM)


def feed(kernel, in_specs, outs, scratch, hidden, width, flops, vmem, *operands):
    moved = sum(x.size * x.dtype.itemsize for x in (*operands, *outs))
    return pl.pallas_call(
        kernel,
        in_specs=in_specs,
        out_specs=(HBM_SPEC, *[VMEM_SPEC] * (len(outs) - 1)),
        out_shape=tuple(outs),
        scratch_shapes=[
            *scratch,
            pltpu.VMEM((3, width // (2 * HALF), 2, HALF, hidden), BF),
            pltpu.SemaphoreType.DMA((3, 2)),
            *[pltpu.SemaphoreType.DMA((3,))] * len(scratch),
        ],
        compiler_params=pltpu.CompilerParams(vmem_limit_bytes=vmem * 2**20),
        cost_estimate=pl.CostEstimate(flops=flops, bytes_accessed=moved, transcendentals=0),
    )(*operands)


def feed_forward(core, ffn_in, own, other):
    rows, width = ffn_in.shape
    hidden = own.shape[-1]
    return feed(
        feed_forward_kernel,
        [SMEM_SPEC, VMEM_SPEC, HBM_SPEC, HBM_SPEC],
        [jax.ShapeDtypeStruct((2, rows, hidden), F32), jax.ShapeDtypeStruct(ffn_in.shape, BF)],
        [pltpu.VMEM((2, rows, hidden), F32)],
        hidden, width, 6 * rows * width * hidden, FEED_VMEM,
        core, ffn_in, own, other,
    )


def feed_backward(core, grad_low, own, other, acts):
    rows, width = grad_low.shape
    hidden = own.shape[-1]
    return feed(
        feed_backward_kernel,
        [SMEM_SPEC, VMEM_SPEC, HBM_SPEC, HBM_SPEC, HBM_SPEC],
        [jax.ShapeDtypeStruct((3, rows, hidden), BF), jax.ShapeDtypeStruct(grad_low.shape, BF)],
        [pltpu.VMEM((2, rows, hidden), F32), pltpu.VMEM((3, rows, hidden), BF)],
        hidden, width, 6 * rows * width * hidden, FEED_VMEM,
        core, grad_low, own, other, acts,
    )


def feed_both(core, ffn_in, grad_low, own, other):
    rows, width = grad_low.shape
    hidden = own.shape[-1]
    out = jax.ShapeDtypeStruct(grad_low.shape, BF)
    return feed(
        feed_both_kernel,
        [SMEM_SPEC, VMEM_SPEC, VMEM_SPEC, HBM_SPEC, HBM_SPEC],
        [jax.ShapeDtypeStruct((3, rows, hidden), BF), out, out],
        [pltpu.VMEM((3, rows, hidden), BF)],
        hidden, width, 12 * rows * width * hidden, FEED_VMEM,
        core, ffn_in, grad_low, own, other,
    )


FEED_VMEM = 58


def feed_weights(core, ffn_in, grad_low, parts):
    rows, width = ffn_in.shape
    hidden = parts.shape[-1]
    blocks = width // (2 * HALF)
    out = jax.ShapeDtypeStruct((blocks, 3 * HALF, hidden), BF)
    out_spec = pl.BlockSpec((blocks, HALF, hidden), lambda k: (0, k, 0))
    return pl.pallas_call(
        feed_weights_kernel,
        grid=(3,),
        in_specs=[
            SMEM_SPEC,
            VMEM_SPEC,
            VMEM_SPEC,
            pl.BlockSpec((1, rows, hidden), lambda k: (k, 0, 0)),
        ],
        out_specs=(out_spec, out_spec),
        out_shape=(out, out),
        scratch_shapes=[
            pltpu.VMEM((width, rows), BF),
            pltpu.VMEM((width, rows), BF),
            pltpu.VMEM((blocks, 2, HALF, hidden), BF),
        ],
        compiler_params=pltpu.CompilerParams(
            dimension_semantics=("arbitrary",), vmem_limit_bytes=FEED_VMEM * 2**20
        ),
        cost_estimate=pl.CostEstimate(flops=2**20, bytes_accessed=2**20, transcendentals=0),
    )(core, ffn_in, grad_low, parts)


def per_device(
    tokens,
    cotangent,
    segment_ids,
    mixer_gain,
    ffn_gain,
    gate_master,
    up_master,
    down_master,
    conv_in,
    conv_kernel,
    conv_out,
    query_master,
    key_master,
    value_master,
    query_gain,
    key_gain,
    output_master,
):
    core = lax.axis_index("pipe")
    lane = lax.axis_index("tensor")
    at_dp = lax.axis_index("dp_0") * 4 + lax.axis_index("dp_1")
    seq_len, width = tokens.shape
    rows = seq_len // 2
    shard = rows // 4
    channels = conv_kernel.shape[1]
    head_dim = query_gain.shape[0]
    hidden_width = gate_master.shape[2]
    dp_rows = gate_master.shape[1]
    mix_rows = conv_in.shape[0]
    attn_cols = 3 * channels
    segments = segment_ids[0]

    core_at = core.astype(jnp.int32).reshape(1)
    dense_shard = jnp.stack([gate_master[0], up_master[0], down_master[0].T]).astype(BF)
    dense_shard = dense_shard.reshape(3, 2, HALF, hidden_width)
    keep = lax.dynamic_index_in_dim(dense_shard, core, 1, False).reshape(3 * HALF, hidden_width)
    send = lax.dynamic_index_in_dim(dense_shard, 1 - core, 1, False).reshape(3 * HALF, hidden_width)
    got = other_core(send)
    attn_shard = jnp.concatenate([query_master, key_master, value_master, output_master.T], axis=1)
    attn_shard = jnp.pad(attn_shard.astype(BF), ((0, 0), (0, hidden_width - attn_cols)))
    own0 = jnp.concatenate([jnp.where(core == 0, keep, got), attn_shard], axis=0)
    own0 = lax.all_gather(own0, DP, axis=0, tiled=False)
    own1 = lax.all_gather(jnp.where(core == 0, got, keep), DP, axis=0, tiled=False)

    conv_shard = jnp.concatenate(
        [conv_in.reshape(mix_rows, 3 * channels), conv_out.T], axis=1
    ).astype(BF)
    gains = jnp.concatenate([mixer_gain, ffn_gain], 1).astype(BF)
    conv_shard = jnp.concatenate(
        [conv_shard, jnp.pad(gains, ((0, 7), (0, width - 2 * dp_rows)))], axis=0
    )
    conv_half = exchange(jnp.broadcast_to(conv_shard[None], (16, *conv_shard.shape)), DP)
    conv_other = other_core(conv_half)

    def rows_of(half):
        return half[:, :mix_rows].reshape(width // 2, width)

    def gains_of(half):
        return half[:, mix_rows, : 2 * dp_rows].reshape(16, 2, dp_rows).swapaxes(0, 1).reshape(2, width)

    conv_whole = in_core_order(core, rows_of(conv_half), rows_of(conv_other))
    conv_in_w, conv_out_t = conv_whole[:, : 3 * channels], conv_whole[:, 3 * channels :]
    gains = in_core_order(core, gains_of(conv_half), gains_of(conv_other)).astype(F32)
    gain_mix, gain_ffn = (gains[0], gains[2]), (gains[1], gains[3])

    start = core * rows
    shard_start = start + lane * shard

    def shard_of(value):
        return lax.dynamic_slice_in_dim(value, shard_start, shard, 0).astype(F32)

    own_segments = lax.dynamic_slice_in_dim(segments, start, rows, 0)
    near = jnp.concatenate(
        [jnp.full((HALO,), -1, jnp.int32), segments, jnp.full((HALO,), -2, jnp.int32)]
    )
    near = lax.dynamic_slice_in_dim(near, start, rows + 2 * HALO, 0)

    padded = jnp.pad(tokens, ((HALO, HALO), (0, 0)))
    window = lax.dynamic_slice_in_dim(padded, start, rows + 2 * HALO, 0)
    normed0, scale_mix0 = rms_forward(window.astype(F32), gain_mix[0])
    normed0 = normed0.astype(BF)
    projected = dot(normed0, conv_in_w)
    in_gate = projected[:, :channels]
    out_gate = projected[:, channels : 2 * channels]
    signal = projected[:, 2 * channels :]
    product = in_gate * signal

    def same(back, count):
        return (near[HALO : HALO + count] == near[HALO - back : HALO - back + count])[:, None]

    total = jnp.zeros((rows, channels), F32)
    for back in range(3):
        moved = product[HALO - back : HALO - back + rows]
        total = total + conv_kernel[2 - back] * jnp.where(same(back, rows), moved, 0.0)
    convolved = (out_gate[HALO : HALO + rows] * total).astype(BF)
    partial = dot_cols(convolved, conv_out_t).astype(BF)
    hidden0 = shard_of(tokens) + scatter_sum(partial, "tensor")
    ffn_in0, scale_ffn0 = rms_forward(hidden0, gain_ffn[0])
    ffn_in0 = ffn_in0.astype(BF)
    own0 = after(own0, hidden0)
    other0 = other_core(own0)
    ffn_in0 = gather(ffn_in0, "tensor")
    acts0, partial = feed_forward(core_at, ffn_in0, own0, other0)
    attn_whole = in_core_order(
        core,
        own0[:, 3 * HALF :, :attn_cols].reshape(width // 2, attn_cols),
        other0[:, 3 * HALF :, :attn_cols].reshape(width // 2, attn_cols),
    )
    qkv_w, output_t = attn_whole[:, : 2 * channels], attn_whole[:, 2 * channels :]
    passed_shard = (hidden0 + scatter_sum(partial, "tensor")).astype(BF)
    passed = gather(passed_shard, "tensor")

    cosine, sine = rotation(positions_of(segments), head_dim)
    cosine = lax.dynamic_slice_in_dim(cosine, start, rows, 0)
    sine = lax.dynamic_slice_in_dim(sine, start, rows, 0)
    head_gains = jnp.stack([jnp.tile(query_gain, 2), jnp.tile(key_gain, 2)])
    head_gains = jnp.pad(head_gains, ((0, 6), (0, 0)))
    before = jnp.where(core == 0, -1, segments[:rows])
    key_column = jnp.broadcast_to(
        jnp.concatenate([before, own_segments])[:, None], (2 * rows, 128)
    )
    query_row = jnp.broadcast_to(own_segments[None, :], (8, rows))

    normed1, scale_mix1 = rms_forward(passed.astype(F32), gain_mix[1])
    normed1 = normed1.astype(BF)
    raw = dot(normed1, qkv_w)
    (low,) = whole(
        rope_forward_kernel,
        [jax.ShapeDtypeStruct((rows, 512), BF)],
        raw,
        cosine,
        sine,
        head_gains,
        vmem=16,
    )
    before_kv = lax.ppermute(low[:, 256:], "pipe", [(0, 1)])
    attended, logs = whole(
        attend_forward_kernel,
        [jax.ShapeDtypeStruct((rows, 256), BF), jax.ShapeDtypeStruct((8, rows), F32)],
        low,
        before_kv,
        key_column,
        query_row,
        scratch=[pltpu.VMEM((2 * rows, 256), BF)],
        flops=4 * 4 * rows * SPAN * 64,
        vmem=32,
    )
    partial = dot_cols(attended, output_t).astype(BF)
    hidden1 = passed_shard.astype(F32) + scatter_sum(partial, "tensor")
    ffn_in1, scale_ffn1 = rms_forward(hidden1, gain_ffn[1])
    ffn_in1 = ffn_in1.astype(BF)
    own1 = after(own1, hidden1)
    other1 = other_core(own1)
    ffn_in1 = gather(ffn_in1, "tensor")
    grad_low = lax.dynamic_slice_in_dim(cotangent, start, rows, 0)
    parts1, second, partial = feed_both(core_at, ffn_in1, grad_low, own1, other1)
    second = lax.psum_scatter(second, "tensor", scatter_dimension=0, tiled=True)
    second = lax.all_gather(
        (hidden1 + second.astype(F32)).astype(BF), "tensor", axis=0, tiled=True
    )
    swapped = other_core(jnp.where(core == 0, second, passed))
    section_output = in_core_order(core, jnp.where(core == 0, passed, second), swapped)

    def gain_sum(value, scale, grad):
        return jnp.sum(grad * value * scale, axis=0)

    grad_ffn_in = scatter_sum(partial, "tensor")
    keep1, send1 = feed_weights(core_at, ffn_in1, grad_low, parts1)
    sum1 = (keep1.astype(F32) + other_core(send1)).astype(BF)
    sum1 = sum1.reshape(-1, hidden_width)
    sum1 = lax.psum_scatter(sum1, DP, scatter_dimension=0, tiled=True)
    ffn_gain1 = gain_sum(hidden1, scale_ffn1, grad_ffn_in)
    grad_hidden = shard_of(cotangent) + rms_backward(hidden1, scale_ffn1, gain_ffn[1], grad_ffn_in)
    hidden_low = gather(grad_hidden.astype(BF), "tensor")
    grad_output_t = dot_rows(hidden_low, attended).astype(BF)
    grad_attended = dot(hidden_low, output_t).astype(BF)
    grad_query, grad_kv = whole(
        attend_backward_kernel,
        [jax.ShapeDtypeStruct((rows, 256), F32), jax.ShapeDtypeStruct((2 * rows, 256), F32)],
        low,
        before_kv,
        key_column,
        query_row,
        logs,
        grad_attended,
        scratch=[pltpu.VMEM((2 * rows, 256), BF)],
        flops=10 * 4 * rows * SPAN * 64,
        vmem=40,
    )
    more_kv = lax.ppermute(grad_kv[:rows], "pipe", [(1, 0)])
    grad_qkv, head_sums = whole(
        rope_backward_kernel,
        [jax.ShapeDtypeStruct((rows, 512), BF), jax.ShapeDtypeStruct((8, 128), F32)],
        raw,
        grad_query,
        grad_kv[rows:],
        more_kv,
        cosine,
        sine,
        head_gains,
        vmem=20,
    )
    partial = dot_cols(grad_qkv, qkv_w)
    mix_gain1 = jnp.sum(partial * passed.astype(F32) * scale_mix1, axis=0)
    grad_normed = scatter_sum(partial.astype(BF), "tensor")
    passed_f32 = passed_shard.astype(F32)
    scale_shard = lax.dynamic_slice_in_dim(scale_mix1, lane * shard, shard, 0)
    grad_passed = grad_hidden + rms_backward(passed_f32, scale_shard, gain_mix[1], grad_normed)
    grad_shard = grad_passed.astype(BF)
    grad_low = gather(grad_shard, "tensor")
    grad_passed = grad_low

    parts0, partial = feed_backward(core_at, grad_low, own0, other0, acts0)
    grad_ffn_in = scatter_sum(partial, "tensor")
    keep0, send0 = feed_weights(core_at, ffn_in0, grad_low, parts0)
    ffn_gain0 = gain_sum(hidden0, scale_ffn0, grad_ffn_in)
    grad_hidden = grad_shard.astype(F32) + rms_backward(
        hidden0, scale_ffn0, gain_ffn[0], grad_ffn_in
    )

    grad_attn = jnp.concatenate(
        [dot_rows(normed1, grad_qkv).astype(BF), grad_output_t], axis=1
    )

    attn_sum = half_of(grad_attn, core).astype(F32) + other_core(half_of(grad_attn, 1 - core))
    attn_sum = attn_sum.astype(BF).reshape(16, mix_rows, attn_cols)
    attn_sum = jnp.pad(attn_sum, ((0, 0), (0, 0), (0, hidden_width - attn_cols)))
    sum0 = (keep0.astype(F32) + other_core(send0)).astype(BF)
    sum0 = jnp.concatenate([sum0, attn_sum], axis=1)
    hidden_low = gather(grad_hidden.astype(BF), "tensor")
    sum0 = after(sum0.reshape(-1, hidden_width), hidden_low)
    sum0 = lax.psum_scatter(sum0, DP, scatter_dimension=0, tiled=True)
    grad_attn = sum0[3 * HALF :, :attn_cols].astype(F32)
    sum0 = sum0[: 3 * HALF]
    mine = jnp.where(core == 0, sum0, sum1).reshape(3, HALF, hidden_width)
    theirs = other_core(jnp.where(core == 0, sum1, sum0)).reshape(3, HALF, hidden_width)
    grad_gate, grad_up, grad_down = (
        in_core_order(core, mine[k], theirs[k]).astype(F32) for k in range(3)
    )

    following = lax.ppermute(hidden_low[:HALO], "pipe", [(1, 0)])
    hidden_more = jnp.concatenate([hidden_low, following], 0)
    grad_out_t = dot_rows(hidden_low, convolved).astype(BF)
    grad_convolved = dot(hidden_more, conv_out_t)
    grad_out_gate = grad_convolved[:rows] * total
    grad_total = grad_convolved * out_gate[HALO:]
    grad_product = jnp.zeros((rows, channels), F32)
    taps = []
    for back in range(3):
        mask = (near[HALO + back : HALO + back + rows] == near[HALO : HALO + rows])[:, None]
        grad_product = grad_product + conv_kernel[2 - back] * jnp.where(
            mask, grad_total[back : back + rows], 0.0
        )
        moved = product[HALO - back : HALO - back + rows]
        taps.append(jnp.sum(jnp.where(same(back, rows), grad_total[:rows] * moved, 0.0), axis=0))
    taps = jnp.stack(taps[::-1])
    own = slice(HALO, HALO + rows)
    grad_projected = jnp.concatenate(
        [grad_product * signal[own], grad_out_gate, grad_product * in_gate[own]], axis=1
    ).astype(BF)
    grad_conv = jnp.concatenate(
        [dot_rows(normed0[own], grad_projected).astype(BF), grad_out_t], axis=1
    )
    partial = dot_cols(grad_projected, conv_in_w)
    mix_gain0 = jnp.sum(partial * window[own].astype(F32) * scale_mix0[own], axis=0)

    taps_wide = lax.dynamic_update_slice_in_dim(
        jnp.zeros((3, width), F32), taps, lane * channels, 1
    )
    heads = (head_sums[:2, :64] + head_sums[:2, 64:]).reshape(1, 128)
    small = jnp.concatenate(
        [
            jnp.stack([mix_gain0, ffn_gain0, mix_gain1, ffn_gain1]),
            taps_wide,
            jnp.pad(heads, ((0, 0), (0, width - 128))),
        ],
        0,
    )

    def two_terms(value):
        high = value.astype(BF)
        return jnp.concatenate([high, (value - high.astype(F32)).astype(BF)], 0)

    def one_term(value):
        return value[:8] + value[8:]

    def sum_beside(blocks, small, axis):
        terms = jnp.broadcast_to(two_terms(small)[None], (blocks.shape[0], 16, width))
        parts = exchange(jnp.concatenate([blocks.astype(BF), terms], 1), axis)
        summed = jnp.sum(parts.astype(F32), axis=0)
        return summed[:-16], one_term(summed[-16:])

    terms = exchange(jnp.broadcast_to(two_terms(small)[None], (4, 16, width)), "tensor")
    small = one_term(jnp.sum(terms.astype(F32), axis=0))
    small = small + one_term(other_core(two_terms(small)).astype(F32))

    grad_normed = direct_scatter_sum(partial.astype(BF), "tensor")
    tokens_shard = shard_of(tokens)
    scale_shard = lax.dynamic_slice_in_dim(scale_mix0, HALO + lane * shard, shard, 0)
    grad_tokens = grad_hidden + rms_backward(tokens_shard, scale_shard, gain_mix[0], grad_normed)
    grad_tokens = direct_gather(grad_tokens.astype(BF), "tensor")
    swapped = other_core(jnp.where(core == 0, grad_passed, grad_tokens))
    input_grad = in_core_order(
        core, jnp.where(core == 0, grad_tokens, grad_passed), swapped
    ).astype(F32)

    blocks = half_of(grad_conv, core).astype(F32) + other_core(half_of(grad_conv, 1 - core))
    blocks, small = sum_beside(blocks.reshape(16, mix_rows, width), small, DP)

    def own_gain(pair):
        return lax.dynamic_slice(pair, (core, at_dp * dp_rows), (1, dp_rows))

    return (
        section_output[None],
        input_grad[None],
        own_gain(small[0:4:2]),
        own_gain(small[1:4:2]),
        grad_gate[None],
        grad_up[None],
        grad_down.T[None],
        blocks[:, : 3 * channels].reshape(mix_rows, 3, channels),
        small[4:7],
        blocks[:, 3 * channels :].T,
        grad_attn[:, :channels],
        grad_attn[:, channels : channels + 128],
        grad_attn[:, channels + 128 : 2 * channels],
        small[7, :64],
        small[7, 64:128],
        grad_attn[:, 2 * channels :].T,
    )


def solution(mesh):
    finer = Mesh(
        mesh.devices.reshape(mesh.shape["pipe"], mesh.shape["tensor"], 4, 4),
        ("pipe", "tensor", "dp_0", "dp_1"),
    )
    return jax.shard_map(
        per_device,
        mesh=finer,
        in_specs=(
            P(DP, None),
            P(DP, None),
            P(DP, None),
            P("pipe", DP),
            P("pipe", DP),
            P("pipe", DP, "tensor"),
            P("pipe", DP, "tensor"),
            P("pipe", "tensor", DP),
            P(PIPE_DP, None, "tensor"),
            P(None, "tensor"),
            P("tensor", PIPE_DP),
            P(PIPE_DP, "tensor"),
            P(PIPE_DP, "tensor"),
            P(PIPE_DP, "tensor"),
            P(),
            P(),
            P("tensor", PIPE_DP),
        ),
        out_specs=(
            P("pipe", DP, None),
            P("pipe", DP, None),
            P("pipe", DP),
            P("pipe", DP),
            P("pipe", DP, "tensor"),
            P("pipe", DP, "tensor"),
            P("pipe", "tensor", DP),
            P(PIPE_DP, None, "tensor"),
            P(),
            P("tensor", PIPE_DP),
            P(PIPE_DP, "tensor"),
            P(PIPE_DP, "tensor"),
            P(PIPE_DP, "tensor"),
            P(),
            P(),
            P("tensor", PIPE_DP),
        ),
        check_vma=False,
    )
```

profile of v0, /device:TPU:1, one launch (start us, length us, event | category | flops | bytes accessed | tf_op | source)
XLA Modules:
  0.0 499.8 jit_solution(4289228200570606877)
XLA Ops:
  14.9 30.2 %all_to_all.75 = bf16[16,40,1024]{2,1,0:T(8,128)(2,1)S(1)} all-to-all(bf16[16,40,1024]{2,1,0:T(8,128)(2,1)S(1)} %broadcast_in_dim.167), channel_id=1, replica_groups=mesh['pipe'=2,'tensor'=4,'dp_0'=4,'dp_1'=4] {'dp_0','dp_1'}, dimensions={0} | all-to-all | bytes 2621440 | tf_op jit(solution)/shard_map/all_to_all | solution.py:34
  58.2 5.0 %all-to-all-start.1 = ((bf16[4,128,1024]{2,1,0:T(8,128)(2,1)}), bf16[4,128,1024]{2,1,0:T(8,128)(2,1)S(1)}, u32[]{:S(2)}, u32[]{:S(2)}) async-start(bf16[4,128,1024]{2,1,0:T(8,128)(2,1)} %bitcast.10), calls=%async_computation.1 | async-start | bytes 2097152 | tf_op jit(solution)/shard_map/all_to_all | solution.py:34
  63.2 14.5 %all-to-all-done.1 = bf16[4,128,1024]{2,1,0:T(8,128)(2,1)S(1)} async-done(((bf16[4,128,1024]{2,1,0:T(8,128)(2,1)}), bf16[4,128,1024]{2,1,0:T(8,128)(2,1)S(1)}, u32[]{:S(2)}, u32[]{:S(2)}) %all-to-all-start.1) | async-done | bytes 1048608 | tf_op jit(solution)/shard_map/all_to_all | solution.py:34
  80.0 18.1 %all_to_all.76 = bf16[4,128,1024]{2,1,0:T(8,128)(2,1)} all-to-all(bf16[4,128,1024]{2,1,0:T(8,128)(2,1)S(1)} %broadcast_in_dim.171), channel_id=1, replica_groups=mesh['pipe'=2,'tensor'=4,'dp_0'=4,'dp_1'=4] {'tensor'}, dimensions={0} | all-to-all | bytes 2097152 | tf_op jit(solution)/shard_map/all_to_all | solution.py:34
  98.1 9.2 %shard_map.288 = (f32[2,512,1152]{2,1,0:T(8,128)}, bf16[512,1024]{1,0:T(8,128)(2,1)}) custom-call(s32[1]{0:T(128)} %bitcast.11.core_ref, bf16[512,1024]{1,0:T(8,128)(2,1)} %bitcast.155, bf16[16,128,1152]{2,1,0:T(8,128)(2,1)} %bitcast.141, bf16[16,128,1152]{2,1,0:T(8,128)(2,1)} %collective-permute-done.2.other_ref), custom_call_target="tpu_custom_call" | custom-call | flops 3623878656 | bytes 16252932 | tf_op jit(solution)/shard_map/pallas_call | solution.py:416
  107.2 3.6 all-to-all-start.3
  111.4 13.4 %all-to-all-done.3 = bf16[4,128,1024]{2,1,0:T(8,128)(2,1)S(1)} async-done(((bf16[4,128,1024]{2,1,0:T(8,128)(2,1)}), bf16[4,128,1024]{2,1,0:T(8,128)(2,1)S(1)}, u32[]{:S(2)}, u32[]{:S(2)}) %all-to-all-start.3) | async-done | bytes 1048608 | tf_op jit(solution)/shard_map/all_to_all | solution.py:34
  126.9 3.7 all-to-all-start.4
  135.1 8.6 %all-to-all-done.4 = bf16[4,128,1024]{2,1,0:T(8,128)(2,1)S(1)} async-done(((bf16[4,128,1024]{2,1,0:T(8,128)(2,1)}), bf16[4,128,1024]{2,1,0:T(8,128)(2,1)S(1)}, u32[]{:S(2)}, u32[]{:S(2)}) %all-to-all-start.4) | async-done | bytes 1048608 | tf_op jit(solution)/shard_map/all_to_all | solution.py:34
  149.2 3.9 collective-permute-done.3.before_ref
  153.3 5.4 %shard_map.290 = (bf16[512,256]{1,0:T(8,128)(2,1)S(1)}, f32[8,512]{1,0:T(8,128)S(1)}) custom-call(bf16[512,512]{1,0:T(8,128)(2,1)S(1)} %shard_map.289.own_ref, bf16[512,256]{1,0:T(8,128)(2,1)S(1)} %collective-permute-done.3.before_ref, s32[1024,128]{1,0:T(8,128)S(1)} %broadcast_in_dim.174.column_ref, s32[8,512]{1,0:T(8,128)S(1)} %broadcast_in_dim.175.row_ref), custom_call_target="tpu_custom_call" | custom-call | flops 402653184 | bytes 1605632 | tf_op jit(solution)/shard_map/pallas_call | solution.py:122
  160.3 17.4 %all_to_all.77 = bf16[4,128,1024]{2,1,0:T(8,128)(2,1)S(1)} all-to-all(bf16[4,128,1024]{2,1,0:T(8,128)(2,1)S(1)} %bitcast.154), channel_id=1, replica_groups=mesh['pipe'=2,'tensor'=4,'dp_0'=4,'dp_1'=4] {'tensor'}, dimensions={0} | all-to-all | bytes 2097152 | tf_op jit(solution)/shard_map/all_to_all | solution.py:34
  180.5 4.3 all-to-all-start.6
  187.5 12.6 %all-to-all-done.6 = bf16[4,128,1024]{2,1,0:T(8,128)(2,1)} async-done(((bf16[4,128,1024]{2,1,0:T(8,128)(2,1)}), bf16[4,128,1024]{2,1,0:T(8,128)(2,1)}, u32[]{:S(2)}, u32[]{:S(2)}) %all-to-all-start.6) | async-done | bytes 1048608 | tf_op jit(solution)/shard_map/all_to_all | solution.py:34
  200.1 13.9 %shard_map.291 = (bf16[3,512,1152]{2,1,0:T(8,128)(2,1)}, bf16[512,1024]{1,0:T(8,128)(2,1)}, bf16[512,1024]{1,0:T(8,128)(2,1)}) custom-call(s32[1]{0:T(128)} %bitcast.11.core_ref, bf16[512,1024]{1,0:T(8,128)(2,1)} %bitcast.38.in_ref, bf16[512,1024]{1,0:T(8,128)(2,1)} %constant_dynamic-slice_fusion.4.grad_ref, bf16[16,96,1152]{2,1,0:T(8,128)(2,1)} %bitcast.207, ...), custom_call_target="tpu_custom_call" | custom-call | flops 7247757312 | bytes 14811140 | tf_op jit(solution)/shard_map/pallas_call | solution.py:416
  214.1 4.3 all-to-all-start.7
  218.4 9.7 %shard_map.296 = (bf16[16,96,1152]{2,1,0:T(8,128)(2,1)}, bf16[16,96,1152]{2,1,0:T(8,128)(2,1)}) custom-call(s32[1]{0:T(128)} %bitcast.11.core_ref, bf16[512,1024]{1,0:T(8,128)(2,1)} %bitcast.38.in_ref, bf16[512,1024]{1,0:T(8,128)(2,1)} %constant_dynamic-slice_fusion.4.grad_ref, bf16[3,512,1152]{2,1,0:T(8,128)(2,1)} %get-tuple-element.53.part_ref), custom_call_target="tpu_custom_call" | custom-call | flops 1048576 | bytes 1048576 | tf_op jit(solution)/shard_map/pallas_call | solution.py:481
  228.8 13.2 %all-to-all-done.7 = bf16[4,128,1024]{2,1,0:T(8,128)(2,1)} async-done(((bf16[4,128,1024]{2,1,0:T(8,128)(2,1)}), bf16[4,128,1024]{2,1,0:T(8,128)(2,1)}, u32[]{:S(2)}, u32[]{:S(2)}) %all-to-all-start.7) | async-done | bytes 1048608 | tf_op jit(solution)/shard_map/all_to_all | solution.py:34
  247.0 16.9 %all_to_all.78 = bf16[4,128,1024]{2,1,0:T(8,128)(2,1)S(1)} all-to-all(bf16[4,128,1024]{2,1,0:T(8,128)(2,1)S(1)} %broadcast_in_dim.178), channel_id=1, replica_groups=mesh['pipe'=2,'tensor'=4,'dp_0'=4,'dp_1'=4] {'tensor'}, dimensions={0} | all-to-all | bytes 2097152 | tf_op jit(solution)/shard_map/all_to_all | solution.py:34
  265.7 6.2 %shard_map.292 = (f32[512,256]{1,0:T(8,128)S(1)}, f32[1024,256]{1,0:T(8,128)S(1)}) custom-call(bf16[512,512]{1,0:T(8,128)(2,1)S(1)} %shard_map.289.own_ref, bf16[512,256]{1,0:T(8,128)(2,1)S(1)} %copy-done.3, s32[1024,128]{1,0:T(8,128)S(1)} %broadcast_in_dim.174.column_ref, s32[8,512]{1,0:T(8,128)S(1)} %broadcast_in_dim.175.row_ref, ...), custom_call_target="tpu_custom_call" | custom-call | flops 1006632960 | bytes 3178496 | tf_op jit(solution)/shard_map/pallas_call | solution.py:122
  272.8 3.8 collective-permute-start.6
  282.0 3.5 all-to-all-start.9
  285.6 5.8 %add_convert_fusion = bf16[16,96,1152]{2,1,0:T(8,128)(2,1)} fusion(bf16[16,96,1152]{2,1,0:T(8,128)(2,1)} %collective-permute-done.19, bf16[16,96,1152]{2,1,0:T(8,128)(2,1)} %get-tuple-element.54), kind=kLoop, calls=%fused_computation.2 | loop fusion | flops 7077888 | bytes 10616832 | tf_op jit(solution)/shard_map/convert_element_type | solution.py:673
  291.4 12.7 %all-to-all-done.9 = bf16[4,128,1024]{2,1,0:T(8,128)(2,1)S(1)} async-done(((bf16[4,128,1024]{2,1,0:T(8,128)(2,1)}), bf16[4,128,1024]{2,1,0:T(8,128)(2,1)S(1)}, u32[]{:S(2)}, u32[]{:S(2)}) %all-to-all-start.9) | async-done | bytes 1048608 | tf_op jit(solution)/shard_map/all_to_all | solution.py:34
  304.9 17.5 %all_to_all.79 = bf16[4,128,1024]{2,1,0:T(8,128)(2,1)} all-to-all(bf16[4,128,1024]{2,1,0:T(8,128)(2,1)S(1)} %broadcast_in_dim.179), channel_id=1, replica_groups=mesh['pipe'=2,'tensor'=4,'dp_0'=4,'dp_1'=4] {'tensor'}, dimensions={0} | all-to-all | bytes 2097152 | tf_op jit(solution)/shard_map/all_to_all | solution.py:34
  322.4 12.5 %shard_map.294 = (bf16[3,512,1152]{2,1,0:T(8,128)(2,1)}, bf16[512,1024]{1,0:T(8,128)(2,1)}) custom-call(s32[1]{0:T(128)} %bitcast.11.core_ref, bf16[512,1024]{1,0:T(8,128)(2,1)} %bitcast.137, bf16[16,128,1152]{2,1,0:T(8,128)(2,1)} %bitcast.143, bf16[16,128,1152]{2,1,0:T(8,128)(2,1)} %collective-permute-done.2.other_ref, ...), custom_call_target="tpu_custom_call" | custom-call | flops 3623878656 | bytes 19791876 | tf_op jit(solution)/shard_map/pallas_call | solution.py:416
  334.9 9.7 %shard_map.295 = (bf16[16,96,1152]{2,1,0:T(8,128)(2,1)}, bf16[16,96,1152]{2,1,0:T(8,128)(2,1)}) custom-call(s32[1]{0:T(128)} %bitcast.11.core_ref, bf16[512,1024]{1,0:T(8,128)(2,1)} %bitcast.156, bf16[512,1024]{1,0:T(8,128)(2,1)} %bitcast.138, bf16[3,512,1152]{2,1,0:T(8,128)(2,1)} %get-tuple-element.49.part_ref), custom_call_target="tpu_custom_call" | custom-call | flops 1048576 | bytes 1048576 | tf_op jit(solution)/shard_map/pallas_call | solution.py:481
  348.7 3.8 all-to-all-start.11
  353.8 2.3 add_convert_fusion.3
  356.1 2.4 copy.66
  358.5 8.6 %all-to-all-done.11 = bf16[4,128,1024]{2,1,0:T(8,128)(2,1)S(1)} async-done(((bf16[4,128,1024]{2,1,0:T(8,128)(2,1)}), bf16[4,128,1024]{2,1,0:T(8,128)(2,1)S(1)}, u32[]{:S(2)}, u32[]{:S(2)}) %all-to-all-start.11) | async-done | bytes 1048608 | tf_op jit(solution)/shard_map/all_to_all | solution.py:34
  368.8 3.5 all-to-all-start.12
  372.4 4.1 add_convert_fusion.1
  376.5 2.8 fusion.1
  379.3 6.8 %all-to-all-done.12 = bf16[4,128,1024]{2,1,0:T(8,128)(2,1)S(1)} async-done(((bf16[4,128,1024]{2,1,0:T(8,128)(2,1)}), bf16[4,128,1024]{2,1,0:T(8,128)(2,1)S(1)}, u32[]{:S(2)}, u32[]{:S(2)}) %all-to-all-start.12) | async-done | bytes 1048608 | tf_op jit(solution)/shard_map/all_to_all | solution.py:34
  387.3 2.8 bitcast_select_fusion.3
  401.3 3.3 all-to-all-start.13
  404.7 3.6 convolution_convert_fusion
  409.2 2.9 collective-permute-start.10
  412.4 2.4 collective-permute-start.9
  418.7 6.2 %collective-permute-done.8 = bf16[128,1024]{1,0:T(8,128)(2,1)} collective-permute-done((bf16[128,1024]{1,0:T(8,128)(2,1)}, bf16[128,1024]{1,0:T(8,128)(2,1)}, u32[]{:S(2)}, u32[]{:S(2)}) %collective-permute-start.8) | collective-permute-done | bytes 262176 | tf_op jit(solution)/shard_map/ppermute | solution.py:51
  433.5 4.3 collective-permute-done.11
  439.2 5.7 %collective-permute-done.13 = bf16[128,1024]{1,0:T(8,128)(2,1)S(1)} collective-permute-done((bf16[128,1024]{1,0:T(8,128)(2,1)S(1)}, bf16[128,1024]{1,0:T(8,128)(2,1)S(1)}, u32[]{:S(2)}, u32[]{:S(2)}) %collective-permute-start.13) | collective-permute-done | bytes 262176 | tf_op jit(solution)/shard_map/ppermute | solution.py:51
  448.0 7.1 %all-to-all-start.14 = ((bf16[16,48,1024]{2,1,0:T(8,128)(2,1)}), bf16[16,48,1024]{2,1,0:T(8,128)(2,1)S(1)}, u32[]{:S(2)}, u32[]{:S(2)}) async-start(bf16[16,48,1024]{2,1,0:T(8,128)(2,1)} %pad_maximum_fusion), calls=%async_computation.15 | async-start | bytes 3145728 | tf_op jit(solution)/shard_map/all_to_all | solution.py:34
  455.1 2.8 bitcast_select_fusion.1
  459.7 4.7 maximum_select_fusion.1
  464.4 2.9 fusion.9
  467.3 15.0 %all-to-all-done.14 = bf16[16,48,1024]{2,1,0:T(8,128)(2,1)S(1)} async-done(((bf16[16,48,1024]{2,1,0:T(8,128)(2,1)}), bf16[16,48,1024]{2,1,0:T(8,128)(2,1)S(1)}, u32[]{:S(2)}, u32[]{:S(2)}) %all-to-all-start.14) | async-done | bytes 1572896 | tf_op jit(solution)/shard_map/all_to_all | solution.py:34
  (332 shorter events, 106.5 us)
Async XLA Ops:
  7.2 70.8 %all-gather.8.cloned.1.call-start = ((), (), s32[]{:S(2)}) async-start(), calls=%async_computation.22 | async-start | bytes 5013504 | tf_op jit(solution)/shard_map/all_gather | solution.py:546
  10.4 2.6 collective-permute-start.1
  14.7 32.7 %copy-start.44 = (s32[1,1024]{1,0:T(1,128)S(1)}, s32[1,1024]{1,0:T(1,128)}, u32[]{:S(2)}) copy-start(s32[1,1024]{1,0:T(1,128)} %param.19) | copy-start | bytes 12292
  14.7 32.8 %copy-start.12 = (bf16[1024,1024]{1,0:T(8,128)(2,1)S(1)}, bf16[1024,1024]{1,0:T(8,128)(2,1)}, u32[]{:S(2)}) copy-start(bf16[1024,1024]{1,0:T(8,128)(2,1)} %param.17) | copy-start | bytes 6291460
  14.9 33.0 %copy-start.50 = (f32[3,256]{1,0:T(4,128)S(1)}, f32[3,256]{1,0:T(4,128)}, u32[]{:S(2)}) copy-start(f32[3,256]{1,0:T(4,128)} %param.26) | copy-start | bytes 9220
  45.1 5.0 %collective-permute-start = (bf16[16,40,1024]{2,1,0:T(8,128)(2,1)S(1)}, bf16[16,40,1024]{2,1,0:T(8,128)(2,1)}, u32[]{:S(2)}, u32[]{:S(2)}) collective-permute-start(bf16[16,40,1024]{2,1,0:T(8,128)(2,1)S(1)} %all_to_all.75), channel_id=1, source_target_pairs={{0,64},{64,0},{1,65},{65,1},{2,66},{66,2},{3,67},{67,3},{4,68},{68... | collective-permute-start | bytes 3932168 | tf_op jit(solution)/shard_map/ppermute | solution.py:81
  58.2 19.5 %all-to-all-start.1 = ((bf16[4,128,1024]{2,1,0:T(8,128)(2,1)}), bf16[4,128,1024]{2,1,0:T(8,128)(2,1)S(1)}, u32[]{:S(2)}, u32[]{:S(2)}) async-start(bf16[4,128,1024]{2,1,0:T(8,128)(2,1)} %bitcast.10), calls=%async_computation.1 | async-start | bytes 2097152 | tf_op jit(solution)/shard_map/all_to_all | solution.py:34
  63.2 114.8 %all-gather.10.cloned.1.call-start = ((), (), s32[]{:S(2)}) async-start(), calls=%async_computation.23 | async-start | bytes 3760128 | tf_op jit(solution)/shard_map/all_gather | solution.py:547
  78.0 47.0 %copy-start.10 = (f32[128,1024]{1,0:T(8,128)}, f32[128,1024]{1,0:T(8,128)S(1)}, u32[]{:S(2)}) copy-start(f32[128,1024]{1,0:T(8,128)S(1)} %get-tuple-element.131) | copy-start | bytes 1572868
  78.1 20.0 %collective-permute-start.2 = (bf16[16,128,1152]{2,1,0:T(8,128)(2,1)}, bf16[16,128,1152]{2,1,0:T(8,128)(2,1)}, u32[]{:S(2)}, u32[]{:S(2)}) collective-permute-start(bf16[16,128,1152]{2,1,0:T(8,128)(2,1)} %bitcast.140), channel_id=1, source_target_pairs={{0,64},{64,0},{1,65},{65,1},{2,66},{66,2},{3,67},{67,3},{4,68},{68... | collective-permute-start | bytes 14155784 | tf_op jit(solution)/shard_map/ppermute | solution.py:81
  107.2 17.6 %all-to-all-start.3 = ((bf16[4,128,1024]{2,1,0:T(8,128)(2,1)}), bf16[4,128,1024]{2,1,0:T(8,128)(2,1)S(1)}, u32[]{:S(2)}, u32[]{:S(2)}) async-start(bf16[4,128,1024]{2,1,0:T(8,128)(2,1)} %bitcast.165), calls=%async_computation.3 | async-start | bytes 2097152 | tf_op jit(solution)/shard_map/all_to_all | solution.py:34
  126.9 16.8 %all-to-all-start.4 = ((bf16[4,128,1024]{2,1,0:T(8,128)(2,1)}), bf16[4,128,1024]{2,1,0:T(8,128)(2,1)S(1)}, u32[]{:S(2)}, u32[]{:S(2)}) async-start(bf16[4,128,1024]{2,1,0:T(8,128)(2,1)} %broadcast_in_dim.172), calls=%async_computation.4 | async-start | bytes 2097152 | tf_op jit(solution)/shard_map/all_to_all | solution.py:34
  147.9 5.2 %collective-permute-start.3 = (bf16[512,256]{1,0:T(8,128)(2,1)S(1)}, bf16[512,256]{1,0:T(8,128)(2,1)S(1)}, u32[]{:S(2)}, u32[]{:S(2)}) collective-permute-start(bf16[512,256]{1,0:T(8,128)(2,1)S(1)} %slice.338), channel_id=1, source_target_pairs={{0,64},{1,65},{2,66},{3,67},{4,68},{5,69},{6,70},{7,71},{8,72},{9,... | collective-permute-start | bytes 786440 | tf_op jit(solution)/shard_map/ppermute | solution.py:640
  153.1 24.5 %copy-start.2 = (bf16[512,256]{1,0:T(8,128)(2,1)}, bf16[512,256]{1,0:T(8,128)(2,1)S(1)}, u32[]{:S(2)}) copy-start(bf16[512,256]{1,0:T(8,128)(2,1)S(1)} %collective-permute-done.3.before_ref) | copy-start | bytes 786436
  160.2 17.6 %copy-start.15 = (bf16[128,1024]{1,0:T(8,128)(2,1)S(1)}, bf16[128,1024]{1,0:T(8,128)(2,1)}, u32[]{:S(2)}) copy-start(bf16[128,1024]{1,0:T(8,128)(2,1)} %copy-done.14) | copy-start | bytes 786436
  178.0 22.1 %collective-permute-start.4 = (bf16[16,96,1152]{2,1,0:T(8,128)(2,1)}, bf16[16,96,1152]{2,1,0:T(8,128)(2,1)}, u32[]{:S(2)}, u32[]{:S(2)}) collective-permute-start(bf16[16,96,1152]{2,1,0:T(8,128)(2,1)} %bitcast.206), channel_id=1, source_target_pairs={{0,64},{64,0},{1,65},{65,1},{2,66},{66,2},{3,67},{67,3},{4,68},{68... | collective-permute-start | bytes 10616840 | tf_op jit(solution)/shard_map/ppermute | solution.py:81
  180.5 19.6 %all-to-all-start.6 = ((bf16[4,128,1024]{2,1,0:T(8,128)(2,1)}), bf16[4,128,1024]{2,1,0:T(8,128)(2,1)}, u32[]{:S(2)}, u32[]{:S(2)}) async-start(bf16[4,128,1024]{2,1,0:T(8,128)(2,1)} %broadcast_in_dim.176), calls=%async_computation.6 | async-start | bytes 2097152 | tf_op jit(solution)/shard_map/all_to_all | solution.py:34
  184.8 59.7 %reduce-scatter.4.cloned.1.call-start = ((), (), s32[]{:S(2)}) async-start(), calls=%async_computation.18 | async-start | bytes 1310720 | tf_op jit(solution)/shard_map/reduce_scatter | solution.py:661
  214.1 28.0 %all-to-all-start.7 = ((bf16[4,128,1024]{2,1,0:T(8,128)(2,1)}), bf16[4,128,1024]{2,1,0:T(8,128)(2,1)}, u32[]{:S(2)}, u32[]{:S(2)}) async-start(bf16[4,128,1024]{2,1,0:T(8,128)(2,1)} %bitcast.164), calls=%async_computation.8 | async-start | bytes 2097152 | tf_op jit(solution)/shard_map/all_to_all | solution.py:34
  218.3 168.1 %all-gather.6.cloned.1.call-start = ((), (), s32[]{:S(2)}) async-start(), calls=%async_computation.19 | async-start | bytes 1310720 | tf_op jit(solution)/shard_map/all_gather | solution.py:662
  228.1 57.5 %collective-permute-start.19 = (bf16[16,96,1152]{2,1,0:T(8,128)(2,1)}, bf16[16,96,1152]{2,1,0:T(8,128)(2,1)}, u32[]{:S(2)}, u32[]{:S(2)}) collective-permute-start(bf16[16,96,1152]{2,1,0:T(8,128)(2,1)} %get-tuple-element.55), channel_id=1, source_target_pairs={{0,64},{64,0},{1,65},{65,1},{2,66},{66,2},{3,67},{67,3},{4,68},{68... | collective-permute-start | bytes 10616840 | tf_op jit(solution)/shard_map/ppermute | solution.py:81
  246.9 18.8 %copy-start.3 = (bf16[512,256]{1,0:T(8,128)(2,1)S(1)}, bf16[512,256]{1,0:T(8,128)(2,1)}, u32[]{:S(2)}) copy-start(bf16[512,256]{1,0:T(8,128)(2,1)} %copy-done.2) | copy-start | bytes 786436
  272.8 5.5 %collective-permute-start.6 = (f32[512,256]{1,0:T(8,128)}, f32[512,256]{1,0:T(8,128)S(1)}, u32[]{:S(2)}, u32[]{:S(2)}) collective-permute-start(f32[512,256]{1,0:T(8,128)} %get-tuple-element.145), channel_id=1, source_target_pairs={{64,0},{65,1},{66,2},{67,3},{68,4},{69,5},{70,6},{71,7},{72,8},{73... | collective-permute-start | bytes 1572872 | tf_op jit(solution)/shard_map/ppermute | solution.py:694
  282.0 22.2 %all-to-all-start.9 = ((bf16[4,128,1024]{2,1,0:T(8,128)(2,1)}), bf16[4,128,1024]{2,1,0:T(8,128)(2,1)S(1)}, u32[]{:S(2)}, u32[]{:S(2)}) async-start(bf16[4,128,1024]{2,1,0:T(8,128)(2,1)} %bitcast.46), calls=%async_computation.10 | async-start | bytes 2097152 | tf_op jit(solution)/shard_map/all_to_all | solution.py:34
  285.5 200.7 %reduce-scatter.8.cloned.1.call-start = ((), (), s32[]{:S(2)}) async-start(), calls=%async_computation.21 | async-start | bytes 3760128 | tf_op jit(solution)/shard_map/reduce_scatter | solution.py:675
  291.4 13.0 %copy-start.16 = (bf16[128,1024]{1,0:T(8,128)(2,1)S(1)}, bf16[128,1024]{1,0:T(8,128)(2,1)}, u32[]{:S(2)}) copy-start(bf16[128,1024]{1,0:T(8,128)(2,1)} %copy-done.14) | copy-start | bytes 786436
  291.4 13.2 %copy-start.35 = (f32[128,1024]{1,0:T(8,128)S(1)}, f32[128,1024]{1,0:T(8,128)}, u32[]{:S(2)}) copy-start(f32[128,1024]{1,0:T(8,128)} %get-tuple-element.127) | copy-start | bytes 1572868
  304.8 17.7 %copy-start.30 = (bf16[128,1024]{1,0:T(8,128)(2,1)}, bf16[128,1024]{1,0:T(8,128)(2,1)S(1)}, u32[]{:S(2)}) copy-start(bf16[128,1024]{1,0:T(8,128)(2,1)S(1)} %fusion.35) | copy-start | bytes 786436
  344.6 27.8 %collective-permute-start.17 = (bf16[16,96,1152]{2,1,0:T(8,128)(2,1)}, bf16[16,96,1152]{2,1,0:T(8,128)(2,1)}, u32[]{:S(2)}, u32[]{:S(2)}) collective-permute-start(bf16[16,96,1152]{2,1,0:T(8,128)(2,1)} %get-tuple-element.51), channel_id=1, source_target_pairs={{0,64},{64,0},{1,65},{65,1},{2,66},{66,2},{3,67},{67,3},{4,68},{68... | collective-permute-start | bytes 10616840 | tf_op jit(solution)/shard_map/ppermute | solution.py:81
  348.7 5.1 %collective-permute-start.18 = (bf16[512,768]{0,1:T(8,128)(2,1)}, bf16[512,768]{0,1:T(8,128)(2,1)}, u32[]{:S(2)}, u32[]{:S(2)}) collective-permute-start(bf16[512,768]{0,1:T(8,128)(2,1)} %fusion.25), channel_id=1, source_target_pairs={{0,64},{64,0},{1,65},{65,1},{2,66},{66,2},{3,67},{67,3},{4,68},{68... | collective-permute-start | bytes 2359304 | tf_op jit(solution)/shard_map/ppermute | solution.py:81
  348.7 18.4 %all-to-all-start.11 = ((bf16[4,128,1024]{2,1,0:T(8,128)(2,1)}), bf16[4,128,1024]{2,1,0:T(8,128)(2,1)S(1)}, u32[]{:S(2)}, u32[]{:S(2)}) async-start(bf16[4,128,1024]{2,1,0:T(8,128)(2,1)} %bitcast.163), calls=%async_computation.12 | async-start | bytes 2097152 | tf_op jit(solution)/shard_map/all_to_all | solution.py:34
  368.8 17.3 %all-to-all-start.12 = ((bf16[4,128,1024]{2,1,0:T(8,128)(2,1)}), bf16[4,128,1024]{2,1,0:T(8,128)(2,1)S(1)}, u32[]{:S(2)}, u32[]{:S(2)}) async-start(bf16[4,128,1024]{2,1,0:T(8,128)(2,1)} %broadcast_in_dim.180), calls=%async_computation.13 | async-start | bytes 2097152 | tf_op jit(solution)/shard_map/all_to_all | solution.py:34
  372.4 113.9 %reduce-scatter.6.cloned.1.call-start = ((), (), s32[]{:S(2)}) async-start(), calls=%async_computation.20 | async-start | bytes 5013504 | tf_op jit(solution)/shard_map/reduce_scatter | solution.py:736
  390.2 69.6 %collective-permute-start.5 = (bf16[512,1024]{1,0:T(8,128)(2,1)}, bf16[512,1024]{1,0:T(8,128)(2,1)}, u32[]{:S(2)}, u32[]{:S(2)}) collective-permute-start(bf16[512,1024]{1,0:T(8,128)(2,1)} %get-tuple-element.141), channel_id=1, source_target_pairs={{0,64},{64,0},{1,65},{65,1},{2,66},{66,2},{3,67},{67,3},{4,68},{68... | collective-permute-start | bytes 3145736 | tf_op jit(solution)/shard_map/ppermute | solution.py:81
  392.4 2.8 collective-permute-start.7
  401.3 13.5 %all-to-all-start.13 = ((bf16[4,16,1024]{2,1,0:T(8,128)(2,1)}), bf16[4,16,1024]{2,1,0:T(8,128)(2,1)S(1)}, u32[]{:S(2)}, u32[]{:S(2)}) async-start(bf16[4,16,1024]{2,1,0:T(8,128)(2,1)} %broadcast_in_dim.188), calls=%async_computation.14 | async-start | bytes 262144 | tf_op jit(solution)/shard_map/all_to_all | solution.py:34
  409.2 9.5 %collective-permute-start.10 = (bf16[128,1024]{1,0:T(8,128)(2,1)}, bf16[128,1024]{1,0:T(8,128)(2,1)S(1)}, u32[]{:S(2)}, u32[]{:S(2)}) collective-permute-start(bf16[128,1024]{1,0:T(8,128)(2,1)} %get-tuple-element.143), channel_id=1, source_target_pairs={{0,32},{16,48},{32,0},{48,16},{1,33},{17,49},{33,1},{49,17},{2,34}... | collective-permute-start | bytes 786440 | tf_op jit(solution)/shard_map/ppermute | solution.py:51
  412.1 12.7 %collective-permute-start.8 = (bf16[128,1024]{1,0:T(8,128)(2,1)}, bf16[128,1024]{1,0:T(8,128)(2,1)}, u32[]{:S(2)}, u32[]{:S(2)}) collective-permute-start(bf16[128,1024]{1,0:T(8,128)(2,1)} %get-tuple-element.142), channel_id=1, source_target_pairs={{0,16},{16,32},{32,48},{48,0},{1,17},{17,33},{33,49},{49,1},{2,18}... | collective-permute-start | bytes 786440 | tf_op jit(solution)/shard_map/ppermute | solution.py:51
  412.4 12.5 %collective-permute-start.9 = (bf16[128,1024]{1,0:T(8,128)(2,1)}, bf16[128,1024]{1,0:T(8,128)(2,1)}, u32[]{:S(2)}, u32[]{:S(2)}) collective-permute-start(bf16[128,1024]{1,0:T(8,128)(2,1)} %get-tuple-element.144), channel_id=1, source_target_pairs={{0,48},{16,0},{32,16},{48,32},{1,49},{17,1},{33,17},{49,33},{2,50}... | collective-permute-start | bytes 786440 | tf_op jit(solution)/shard_map/ppermute | solution.py:51
  414.8 2.6 collective-permute-start.16
  417.5 28.1 %collective-permute-start.15 = (bf16[512,1024]{0,1:T(8,128)(2,1)S(1)}, bf16[512,1024]{0,1:T(8,128)(2,1)S(1)}, u32[]{:S(2)}, u32[]{:S(2)}) collective-permute-start(bf16[512,1024]{0,1:T(8,128)(2,1)S(1)} %fusion.18), channel_id=1, source_target_pairs={{0,64},{64,0},{1,65},{65,1},{2,66},{66,2},{3,67},{67,3},{4,68},{68... | collective-permute-start | bytes 3145736 | tf_op jit(solution)/shard_map/ppermute | solution.py:81
  427.3 18.3 %copy-start.17 = (bf16[1024,768]{0,1:T(8,128)(2,1)S(1)}, bf16[1024,768]{0,1:T(8,128)(2,1)}, u32[]{:S(2)}) copy-start(bf16[1024,768]{0,1:T(8,128)(2,1)} %convolution_convert_fusion) | copy-start | bytes 4718596
  429.5 8.3 %collective-permute-start.11 = (bf16[128,1024]{1,0:T(8,128)(2,1)S(1)}, bf16[128,1024]{1,0:T(8,128)(2,1)S(1)}, u32[]{:S(2)}, u32[]{:S(2)}) collective-permute-start(bf16[128,1024]{1,0:T(8,128)(2,1)S(1)} %get-tuple-element.119), channel_id=1, source_target_pairs={{0,16},{16,32},{32,48},{48,0},{1,17},{17,33},{33,49},{49,1},{2,18}... | collective-permute-start | bytes 786440 | tf_op jit(solution)/shard_map/ppermute | solution.py:51
  431.0 7.6 %collective-permute-start.12 = (bf16[128,1024]{1,0:T(8,128)(2,1)S(1)}, bf16[128,1024]{1,0:T(8,128)(2,1)S(1)}, u32[]{:S(2)}, u32[]{:S(2)}) collective-permute-start(bf16[128,1024]{1,0:T(8,128)(2,1)S(1)} %get-tuple-element.119), channel_id=1, source_target_pairs={{0,48},{16,0},{32,16},{48,32},{1,49},{17,1},{33,17},{49,33},{2,50}... | collective-permute-start | bytes 786440 | tf_op jit(solution)/shard_map/ppermute | solution.py:51
  432.3 12.6 %collective-permute-start.13 = (bf16[128,1024]{1,0:T(8,128)(2,1)S(1)}, bf16[128,1024]{1,0:T(8,128)(2,1)S(1)}, u32[]{:S(2)}, u32[]{:S(2)}) collective-permute-start(bf16[128,1024]{1,0:T(8,128)(2,1)S(1)} %get-tuple-element.119), channel_id=1, source_target_pairs={{0,32},{16,48},{32,0},{48,16},{1,33},{17,49},{33,1},{49,17},{2,34}... | collective-permute-start | bytes 786440 | tf_op jit(solution)/shard_map/ppermute | solution.py:51
  448.0 34.3 %all-to-all-start.14 = ((bf16[16,48,1024]{2,1,0:T(8,128)(2,1)}), bf16[16,48,1024]{2,1,0:T(8,128)(2,1)S(1)}, u32[]{:S(2)}, u32[]{:S(2)}) async-start(bf16[16,48,1024]{2,1,0:T(8,128)(2,1)} %pad_maximum_fusion), calls=%async_computation.15 | async-start | bytes 3145728 | tf_op jit(solution)/shard_map/all_to_all | solution.py:34
  457.9 6.5 %collective-permute-start.14 = (bf16[512,1024]{1,0:T(8,128)(2,1)}, bf16[512,1024]{1,0:T(8,128)(2,1)S(1)}, u32[]{:S(2)}, u32[]{:S(2)}) collective-permute-start(bf16[512,1024]{1,0:T(8,128)(2,1)} %get-tuple-element.139), channel_id=1, source_target_pairs={{0,64},{64,0},{1,65},{65,1},{2,66},{66,2},{3,67},{67,3},{4,68},{68... | collective-permute-start | bytes 3145736 | tf_op jit(solution)/shard_map/ppermute | solution.py:81
  487.3 3.5 collective-permute-start.20
  (44 other events, 201.1 us)
Sparse Core Ops, SparseCore 0:
  14.7 61.8 all-gather.7
  79.8 47.9 all-gather.9
  214.2 25.7 reduce-scatter.3
  276.7 19.6 all-gather.5
  300.0 81.2 reduce-scatter.7
  386.2 88.5 reduce-scatter.5
where the time goes:
time: 510 us; the launch traced here: 500 us
  waiting for transfers between devices  132 us (26%)
  blocking collectives  100 us (20%)
  starting transfers between devices  75.6 us (15%)
  Pallas kernels  70.5 us (14%)
  other arithmetic  57.1 us (11%)
  local copies, waits for them, and re-layouts  32.5 us (6%)
  matrix products  16.2 us (3%)
  between operations  15.9 us (3%)
    all_to_all x10, waiting for transfers between devices, exchange(): return lax.all_to_all(parts, axis, 0, 0)  105 us
    all_to_all x5, blocking collectives, exchange(): return lax.all_to_all(parts, axis, 0, 0)  100 us
    all_to_all x10, starting transfers between devices, exchange(): return lax.all_to_all(parts, axis, 0, 0)  42 us
    pallas_call x3, Pallas kernels, feed(): pl.pallas_call(kernel, in_specs=in_specs, out_specs=(HBM_SPEC, *[VMEM_SPE...  35.5 us
    pallas_call x2, Pallas kernels, feed_weights(): pl.pallas_call(feed_weights_kernel, grid=(3,), in_specs=[SMEM_SPEC, VMEM_...  19.5 us
    ppermute x6, waiting for transfers between devices, turned(): lax.ppermute(value, axis, [(i, (i + by) % size) for i in range(size)])  17.1 us
    ppermute x12, starting transfers between devices, other_core(): return lax.ppermute(value, 'pipe', [(0, 1), (1, 0)])  16.4 us
    dot_general x12, matrix products, dot(): lax.dot_general(left, right, (dims, ((), ())), preferred_element_type=F32)  16.2 us
  transfers between devices with their start and end apart: 37, of which 19 were waited for; matrix products, arithmetic and copies ran while one was open for 19% of the time, Pallas kernels for 11%

commit v1 on v0

--- a/solution.py
+++ b/solution.py
@@ -34,6 +34,14 @@
     return lax.all_to_all(parts, axis, 0, 0)
 
 
+def blocks_of(value):
+    return exchange(value.reshape(4, value.shape[0] // 4, value.shape[1]), "tensor")
+
+
+def gathered(copies):
+    return exchange(copies, "tensor").reshape(-1, copies.shape[-1])
+
+
 def scatter_sum(value, axis):
     size = lax.axis_size(axis)
     parts = value.reshape(size, value.shape[0] // size, *value.shape[1:])
@@ -116,18 +124,28 @@
     return jnp.tile(cosine, (1, 4)), jnp.tile(jnp.concatenate([-sine, sine], 1), (1, 2))
 
 
-def whole(kernel, out_shapes, *operands, scratch=(), flops=0, vmem=40):
+def not_before(kernel, operands, needed):
+    skipped = range(operands, operands + needed)
+
+    def body(*refs):
+        kernel(*(ref for k, ref in enumerate(refs) if k not in skipped))
+
+    return body
+
+
+def whole(kernel, out_shapes, *operands, scratch=(), flops=0, vmem=40, needs=()):
+    kernel = not_before(kernel, len(operands), len(needs))
     spec = pl.BlockSpec(memory_space=pltpu.VMEM)
     moved = sum(x.size * x.dtype.itemsize for x in (*operands, *out_shapes))
     return pl.pallas_call(
         kernel,
         out_shape=tuple(out_shapes),
-        in_specs=[spec] * len(operands),
+        in_specs=[spec] * len(operands) + [pl.BlockSpec(memory_space=pl.ANY)] * len(needs),
         out_specs=tuple(spec for _ in out_shapes),
         scratch_shapes=scratch,
         compiler_params=pltpu.CompilerParams(vmem_limit_bytes=vmem * 2**20),
         cost_estimate=pl.CostEstimate(flops=flops, bytes_accessed=moved, transcendentals=0),
-    )(*operands)
+    )(*operands, *needs)
 
 
 def head_mean(value, low):
@@ -383,11 +401,11 @@
         copy.wait()
 
 
-def feed_weights_kernel(
-    core_ref, in_ref, grad_ref, part_ref, keep_ref, send_ref, in_t_ref, grad_t_ref, both_ref
-):
-    core = core_ref[0]
+def feed_weights_kernel(in_ref, grad_ref, part_ref, *refs):
+    more_ref = refs[0] if len(refs) == 5 else None
+    out_ref, done_ref, in_t_ref, grad_t_ref = refs[-4:]
     step = pl.program_id(0)
+    done_ref[...] = jnp.zeros_like(done_ref)
 
     @pl.when(step == 0)
     def _():
@@ -396,26 +414,36 @@
 
     @pl.when(step < 2)
     def _():
-        both_ref[...] = dot(in_t_ref[...], part_ref[0]).astype(BF).reshape(both_ref.shape)
+        out_ref[...] = dot(in_t_ref[...], part_ref[0]).astype(BF).reshape(out_ref.shape)
 
     @pl.when(step == 2)
     def _():
-        both_ref[...] = dot(grad_t_ref[...], part_ref[0]).astype(BF).reshape(both_ref.shape)
-
-    keep_ref[...] = both_ref[:, core]
-    send_ref[...] = both_ref[:, 1 - core]
+        out_ref[...] = dot(grad_t_ref[...], part_ref[0]).astype(BF).reshape(out_ref.shape)
+
+    if more_ref is not None:
+
+        @pl.when(step == 3)
+        def _():
+            out_ref[...] = jnp.zeros_like(out_ref)
+            wide = more_ref.shape[1]
+            blocks = out_ref.shape[0]
+            for part in range(2):
+                rows = more_ref[pl.ds(part * blocks * HALF, blocks * HALF), :]
+                out_ref[:, pl.ds(part * HALF, HALF), pl.ds(0, wide)] = rows.reshape(blocks, HALF, wide)
 
 
 SMEM_SPEC = pl.BlockSpec(memory_space=pltpu.SMEM)
 HBM_SPEC = pl.BlockSpec(memory_space=pltpu.HBM)
+ANY_SPEC = pl.BlockSpec(memory_space=pl.ANY)
 VMEM_SPEC = pl.BlockSpec(memory_space=pltpu.VMEM)
 
 
-def feed(kernel, in_specs, outs, scratch, hidden, width, flops, vmem, *operands):
+def feed(kernel, in_specs, outs, scratch, hidden, width, flops, vmem, *operands, needs=()):
+    kernel = not_before(kernel, len(operands), len(needs))
     moved = sum(x.size * x.dtype.itemsize for x in (*operands, *outs))
     return pl.pallas_call(
         kernel,
-        in_specs=in_specs,
+        in_specs=in_specs + [ANY_SPEC] * len(needs),
         out_specs=(HBM_SPEC, *[VMEM_SPEC] * (len(outs) - 1)),
         out_shape=tuple(outs),
         scratch_shapes=[
@@ -426,7 +454,7 @@
         ],
         compiler_params=pltpu.CompilerParams(vmem_limit_bytes=vmem * 2**20),
         cost_estimate=pl.CostEstimate(flops=flops, bytes_accessed=moved, transcendentals=0),
-    )(*operands)
+    )(*operands, *needs)
 
 
 def feed_forward(core, ffn_in, own, other):
@@ -442,7 +470,7 @@
     )
 
 
-def feed_backward(core, grad_low, own, other, acts):
+def feed_backward(core, grad_low, own, other, acts, needs=()):
     rows, width = grad_low.shape
     hidden = own.shape[-1]
     return feed(
@@ -451,7 +479,7 @@
         [jax.ShapeDtypeStruct((3, rows, hidden), BF), jax.ShapeDtypeStruct(grad_low.shape, BF)],
         [pltpu.VMEM((2, rows, hidden), F32), pltpu.VMEM((3, rows, hidden), BF)],
         hidden, width, 6 * rows * width * hidden, FEED_VMEM,
-        core, grad_low, own, other, acts,
+        core, grad_low, own, other, acts, needs=needs,
     )
 
 
@@ -472,33 +500,298 @@
 FEED_VMEM = 58
 
 
-def feed_weights(core, ffn_in, grad_low, parts):
+def feed_weights(ffn_in, grad_low, parts, more=(), needs=()):
     rows, width = ffn_in.shape
     hidden = parts.shape[-1]
-    blocks = width // (2 * HALF)
-    out = jax.ShapeDtypeStruct((blocks, 3 * HALF, hidden), BF)
-    out_spec = pl.BlockSpec((blocks, HALF, hidden), lambda k: (0, k, 0))
+    blocks, steps = width // (2 * HALF), 3 + len(more)
     return pl.pallas_call(
-        feed_weights_kernel,
-        grid=(3,),
+        not_before(feed_weights_kernel, steps, len(needs)),
+        grid=(steps,),
         in_specs=[
-            SMEM_SPEC,
             VMEM_SPEC,
             VMEM_SPEC,
-            pl.BlockSpec((1, rows, hidden), lambda k: (k, 0, 0)),
+            pl.BlockSpec((1, rows, hidden), lambda k: (jnp.minimum(k, 2), 0, 0)),
+            *[VMEM_SPEC] * len(more),
+            *[ANY_SPEC] * len(needs),
         ],
-        out_specs=(out_spec, out_spec),
-        out_shape=(out, out),
-        scratch_shapes=[
-            pltpu.VMEM((width, rows), BF),
-            pltpu.VMEM((width, rows), BF),
-            pltpu.VMEM((blocks, 2, HALF, hidden), BF),
-        ],
+        out_specs=(
+            pl.BlockSpec((blocks, 2 * HALF, hidden), lambda k: (0, k, 0)),
+            pl.BlockSpec((8, 128), lambda k: (0, 0)),
+        ),
+        out_shape=(
+            shape_of(blocks, 2 * HALF * steps, hidden),
+            shape_of(8, 128, kind=F32),
+        ),
+        scratch_shapes=[pltpu.VMEM((width, rows), BF), pltpu.VMEM((width, rows), BF)],
         compiler_params=pltpu.CompilerParams(
             dimension_semantics=("arbitrary",), vmem_limit_bytes=FEED_VMEM * 2**20
         ),
         cost_estimate=pl.CostEstimate(flops=2**20, bytes_accessed=2**20, transcendentals=0),
-    )(core, ffn_in, grad_low, parts)
+    )(ffn_in, grad_low, parts, *more, *needs)
+
+
+def fetch_conv(core_ref, own_ref, other_ref, weights_ref, sems):
+    core = core_ref[0]
+    rows = pl.ds(0, HALF)
+    return [
+        Moved(ref.at[:, rows, :], weights_ref.at[part], sems.at[side]).start()
+        for side, (ref, part) in enumerate(((own_ref, core), (other_ref, 1 - core)))
+    ]
+
+
+def conv_total(product_ref, near_ref, taps_ref, rows):
+    total = jnp.zeros((rows, product_ref.shape[1]), F32)
+    here = near_ref[pl.ds(HALO, rows), :]
+    for back in range(3):
+        same = here == near_ref[pl.ds(HALO - back, rows), :]
+        moved = jnp.where(same, product_ref[pl.ds(HALO - back, rows), :], 0.0)
+        total = total + taps_ref[pl.ds(2 - back, 1), :] * moved
+    return total
+
+
+def conv_forward_kernel(
+    core_ref, own_ref, other_ref, window_ref, gain_ref, near_ref, taps_ref,
+    projected_ref, normed_ref, convolved_ref, out_ref, weights_ref, product_ref, sems,
+):
+    rows, channels = convolved_ref.shape
+    copies = fetch_conv(core_ref, own_ref, other_ref, weights_ref, sems)
+    value = window_ref[...].astype(F32)
+    scale = lax.rsqrt(jnp.mean(value * value, axis=1, keepdims=True) + EPS)
+    normed = (value * scale * gain_ref[pl.ds(0, 1), :]).astype(BF)
+    normed_ref[...] = normed[HALO : HALO + rows]
+    for copy in copies:
+        copy.wait()
+    weights = weights_ref[...].reshape(-1, weights_ref.shape[-1])
+    projected_ref[...] = dot(normed, weights[:, : 3 * channels])
+    product_ref[...] = (
+        projected_ref[:, pl.ds(0, channels)] * projected_ref[:, pl.ds(2 * channels, channels)]
+    )
+    out_gate = projected_ref[pl.ds(HALO, rows), pl.ds(channels, channels)]
+    convolved_ref[...] = (out_gate * conv_total(product_ref, near_ref, taps_ref, rows)).astype(BF)
+    out_ref[...] = dot_cols(convolved_ref[...], weights[:, 3 * channels :]).astype(BF)
+
+
+def conv_backward_kernel(
+    core_ref, own_ref, other_ref, window_ref, near_ref, taps_ref, projected_ref, hidden_ref, next_ref,
+    grad_ref, out_ref, sums_ref, gain_ref, weights_ref, product_ref, total_ref, sems,
+):
+    rows, channels = hidden_ref.shape[0], taps_ref.shape[1]
+    copies = fetch_conv(core_ref, own_ref, other_ref, weights_ref, sems)
+    product_ref[...] = (
+        projected_ref[:, pl.ds(0, channels)] * projected_ref[:, pl.ds(2 * channels, channels)]
+    )
+    for copy in copies:
+        copy.wait()
+    weights = weights_ref[...].reshape(-1, weights_ref.shape[-1])
+    conv_out_t = weights[:, 3 * channels :]
+    gates = pl.ds(channels, channels)
+    grad_convolved = dot(hidden_ref[...], conv_out_t)
+    total_ref[pl.ds(0, rows), :] = grad_convolved * projected_ref[pl.ds(HALO, rows), gates]
+    total_ref[pl.ds(rows, HALO), :] = (
+        dot(next_ref[...], conv_out_t) * projected_ref[pl.ds(HALO + rows, HALO), gates]
+    )
+    grad_gate = grad_convolved * conv_total(product_ref, near_ref, taps_ref, rows)
+    grad_ref[:, gates] = grad_gate.astype(BF)
+    here = near_ref[pl.ds(HALO, rows), :]
+    own_total = total_ref[pl.ds(0, rows), :]
+    grad_product = jnp.zeros((rows, channels), F32)
+    sums_ref[...] = jnp.zeros_like(sums_ref)
+    for back in range(3):
+        same = here == near_ref[pl.ds(HALO + back, rows), :]
+        moved = jnp.where(same, total_ref[pl.ds(back, rows), :], 0.0)
+        grad_product = grad_product + taps_ref[pl.ds(2 - back, 1), :] * moved
+        same = here == near_ref[pl.ds(HALO - back, rows), :]
+        moved = jnp.where(same, own_total * product_ref[pl.ds(HALO - back, rows), :], 0.0)
+        sums_ref[pl.ds(2 - back, 1), :] = jnp.sum(moved, axis=0, keepdims=True)
+    signal = projected_ref[pl.ds(HALO, rows), pl.ds(2 * channels, channels)]
+    in_gate = projected_ref[pl.ds(HALO, rows), pl.ds(0, channels)]
+    grad_ref[:, pl.ds(0, channels)] = (grad_product * signal).astype(BF)
+    grad_ref[:, pl.ds(2 * channels, channels)] = (grad_product * in_gate).astype(BF)
+    out = dot_cols(grad_ref[...], weights[:, : 3 * channels])
+    out_ref[...] = out.astype(BF)
+    value = window_ref[pl.ds(HALO, rows), :].astype(F32)
+    scale = lax.rsqrt(jnp.mean(value * value, axis=1, keepdims=True) + EPS)
+    gain_ref[...] = jnp.zeros_like(gain_ref)
+    gain_ref[pl.ds(0, 1), :] = jnp.sum(out * value * scale, axis=0, keepdims=True)
+
+
+def conv_weights_kernel(
+    core_ref, normed_ref, hidden_ref, grad_ref, convolved_ref, keep_ref, send_ref, in_t_ref, out_t_ref
+):
+    core = core_ref[0]
+    half, wide = keep_ref.shape[0], grad_ref.shape[1]
+    in_t_ref[...] = normed_ref[...].astype(F32).T.astype(BF)
+    out_t_ref[...] = hidden_ref[...].astype(F32).T.astype(BF)
+    for part, ref in ((1 - core, send_ref), (core, keep_ref)):
+        at = pl.ds(pl.multiple_of(part * half, half), half)
+        ref[:, pl.ds(0, wide)] = dot(in_t_ref[at, :], grad_ref[...]).astype(BF)
+        ref[:, pl.ds(wide, convolved_ref.shape[1])] = dot(
+            out_t_ref[at, :], convolved_ref[...]
+        ).astype(BF)
+
+
+def local(kernel, in_specs, outs, scratch, flops, vmem, *operands, needs=()):
+    kernel = not_before(kernel, len(operands), len(needs))
+    moved = sum(x.size * x.dtype.itemsize for x in (*operands, *outs))
+    return pl.pallas_call(
+        kernel,
+        in_specs=in_specs + [ANY_SPEC] * len(needs),
+        out_specs=tuple(VMEM_SPEC for _ in outs),
+        out_shape=tuple(outs),
+        scratch_shapes=scratch,
+        compiler_params=pltpu.CompilerParams(vmem_limit_bytes=vmem * 2**20),
+        cost_estimate=pl.CostEstimate(flops=flops, bytes_accessed=moved, transcendentals=0),
+    )(*operands, *needs)
+
+
+def conv_scratch(width, channels, rows, sums):
+    return [
+        pltpu.VMEM((2, width // (2 * HALF), HALF, width), BF),
+        pltpu.VMEM((rows + 2 * HALO, channels), F32),
+        *[pltpu.VMEM((rows + HALO, channels), F32)] * sums,
+        pltpu.SemaphoreType.DMA((2,)),
+    ]
+
+
+def shape_of(*shape, kind=BF):
+    return jax.ShapeDtypeStruct(shape, kind)
+
+
+def conv_forward(core, own, other, window, gain, near, taps):
+    rows, width, channels = window.shape[0] - 2 * HALO, window.shape[1], taps.shape[1]
+    return local(
+        conv_forward_kernel,
+        [SMEM_SPEC, HBM_SPEC, HBM_SPEC] + [VMEM_SPEC] * 4,
+        [
+            shape_of(rows + 2 * HALO, 3 * channels, kind=F32),
+            shape_of(rows, width),
+            shape_of(rows, channels),
+            shape_of(rows, width),
+        ],
+        conv_scratch(width, channels, rows, 0),
+        8 * rows * width * channels, 28,
+        core, own, other, window, gain, near, taps,
+    )
+
+
+def conv_backward(core, own, other, window, near, taps, projected, hidden, following, needs):
+    rows, width, channels = hidden.shape[0], hidden.shape[1], taps.shape[1]
+    return local(
+        conv_backward_kernel,
+        [SMEM_SPEC, HBM_SPEC, HBM_SPEC] + [VMEM_SPEC] * 6,
+        [
+            shape_of(rows, 3 * channels),
+            shape_of(rows, width),
+            shape_of(8, channels, kind=F32),
+            shape_of(8, width, kind=F32),
+        ],
+        conv_scratch(width, channels, rows, 1),
+        8 * rows * width * channels, 32,
+        core, own, other, window, near, taps, projected, hidden, following, needs=needs,
+    )
+
+
+def conv_weights(core, normed, hidden, grad, convolved):
+    rows, width = hidden.shape
+    out = shape_of(width // 2, width)
+    return local(
+        conv_weights_kernel,
+        [SMEM_SPEC] + [VMEM_SPEC] * 4,
+        [out, out],
+        [pltpu.VMEM((width, rows), BF)] * 2,
+        2**20, 24,
+        core, normed, hidden, grad, convolved,
+    )
+
+
+def sum_of(parts_ref, rows):
+    total = parts_ref[0, pl.ds(0, rows), :].astype(F32)
+    for k in range(1, 4):
+        total = total + parts_ref[k, pl.ds(0, rows), :].astype(F32)
+    return total
+
+
+def spread(out_ref, value):
+    for k in range(4):
+        out_ref[k] = value
+
+
+def back_kernel(parts_ref, base_ref, value_ref, gain_ref, grad_ref, out_ref, sums_ref):
+    rows = base_ref.shape[0]
+    grad = sum_of(parts_ref, rows)
+    value = value_ref[...].astype(F32)
+    scale = lax.rsqrt(jnp.mean(value * value, axis=1, keepdims=True) + EPS)
+    weighted = grad * gain_ref[pl.ds(0, 1), :]
+    inner = jnp.mean(weighted * value, axis=1, keepdims=True)
+    back = scale * weighted - value * (scale * scale * scale) * inner
+    grad_ref[...] = base_ref[...].astype(F32) + back
+    spread(out_ref, grad_ref[...].astype(BF))
+    sums_ref[...] = jnp.zeros_like(sums_ref)
+    if parts_ref.shape[1] == rows:
+        sums_ref[pl.ds(0, 1), :] = jnp.sum(grad * value * scale, axis=0, keepdims=True)
+    else:
+        for k in range(4):
+            sums_ref[...] += (
+                parts_ref[k, pl.ds(rows, 8), :].astype(F32)
+                + parts_ref[k, pl.ds(rows + 8, 8), :].astype(F32)
+            )
+
+
+def back(parts, base, value, gain, needs=()):
+    rows, width = base.shape
+    return local(
+        back_kernel, [VMEM_SPEC] * 4,
+        [
+            shape_of(rows, width, kind=F32),
+            shape_of(4, rows, width),
+            shape_of(8, width, kind=F32),
+        ],
+        [], 2**20, 16, parts, base, value, gain, needs=needs,
+    )
+
+
+def arrange_kernel(place_ref, own_ref, first_ref, third_ref, second_ref, mine_ref, send_ref):
+    lane, core = place_ref[0], place_ref[1]
+    rows, width = own_ref.shape[0], mine_ref.shape[1]
+    mine = pl.ds(pl.multiple_of(core * width, width), width)
+    send = pl.ds(pl.multiple_of((1 - core) * width, width), width)
+    for by, ref in ((0, own_ref), (1, first_ref), (3, third_ref), (2, second_ref)):
+        at = lax.rem(lane + 4 - by, 4) * rows
+        at = pl.ds(pl.multiple_of(at, rows), rows)
+        mine_ref[at, :] = ref[:, mine]
+        send_ref[at, :] = ref[:, send]
+
+
+def arrange(place, parts, needs):
+    rows, width = parts[0].shape[0], parts[0].shape[1] // 2
+    out = shape_of(4 * rows, width)
+    return local(
+        arrange_kernel, [SMEM_SPEC] + [VMEM_SPEC] * 4, [out, out],
+        [], 2**20, 24, place, *parts, needs=needs,
+    )
+
+
+def last_sums_kernel(parts_ref, in_ref, out_ref, small_ref):
+    rows, wide = in_ref.shape
+    total = parts_ref[0].astype(F32)
+    for k in range(1, parts_ref.shape[0]):
+        total = total + parts_ref[k].astype(F32)
+    in_ref[...] = total[:rows, :wide]
+    out_ref[...] = total[:rows, wide:]
+    small_ref[...] = total[rows : rows + 8] + total[rows + 8 :]
+
+
+def last_sums(parts, wide, needs):
+    rows, width = parts.shape[1] - 16, parts.shape[2]
+    return local(
+        last_sums_kernel, [VMEM_SPEC],
+        [
+            shape_of(rows, wide, kind=F32),
+            shape_of(rows, width - wide, kind=F32),
+            shape_of(8, width, kind=F32),
+        ],
+        [], 2**20, 16, parts, needs=needs,
+    )
 
 
 def per_device(
@@ -556,14 +849,9 @@
     conv_half = exchange(jnp.broadcast_to(conv_shard[None], (16, *conv_shard.shape)), DP)
     conv_other = other_core(conv_half)
 
-    def rows_of(half):
-        return half[:, :mix_rows].reshape(width // 2, width)
-
     def gains_of(half):
         return half[:, mix_rows, : 2 * dp_rows].reshape(16, 2, dp_rows).swapaxes(0, 1).reshape(2, width)
 
-    conv_whole = in_core_order(core, rows_of(conv_half), rows_of(conv_other))
-    conv_in_w, conv_out_t = conv_whole[:, : 3 * channels], conv_whole[:, 3 * channels :]
     gains = in_core_order(core, gains_of(conv_half), gains_of(conv_other)).astype(F32)
     gain_mix, gain_ffn = (gains[0], gains[2]), (gains[1], gains[3])
 
@@ -579,25 +867,15 @@
     )
     near = lax.dynamic_slice_in_dim(near, start, rows + 2 * HALO, 0)
 
+    near = jnp.broadcast_to(near[:, None], (rows + 2 * HALO, channels))
+    taps_in = jnp.pad(conv_kernel, ((0, 5), (0, 0)))
+
     padded = jnp.pad(tokens, ((HALO, HALO), (0, 0)))
     window = lax.dynamic_slice_in_dim(padded, start, rows + 2 * HALO, 0)
-    normed0, scale_mix0 = rms_forward(window.astype(F32), gain_mix[0])
-    normed0 = normed0.astype(BF)
-    projected = dot(normed0, conv_in_w)
-    in_gate = projected[:, :channels]
-    out_gate = projected[:, channels : 2 * channels]
-    signal = projected[:, 2 * channels :]
-    product = in_gate * signal
-
-    def same(back, count):
-        return (near[HALO : HALO + count] == near[HALO - back : HALO - back + count])[:, None]
-
-    total = jnp.zeros((rows, channels), F32)
-    for back in range(3):
-        moved = product[HALO - back : HALO - back + rows]
-        total = total + conv_kernel[2 - back] * jnp.where(same(back, rows), moved, 0.0)
-    convolved = (out_gate[HALO : HALO + rows] * total).astype(BF)
-    partial = dot_cols(convolved, conv_out_t).astype(BF)
+    gain_rows = jnp.broadcast_to(gain_mix[0][None], (8, width))
+    projected, normed0, convolved, partial = conv_forward(
+        core_at, conv_half, conv_other, window, gain_rows, near, taps_in
+    )
     hidden0 = shard_of(tokens) + scatter_sum(partial, "tensor")
     ffn_in0, scale_ffn0 = rms_forward(hidden0, gain_ffn[0])
     ffn_in0 = ffn_in0.astype(BF)
@@ -658,26 +936,22 @@
     ffn_in1 = gather(ffn_in1, "tensor")
     grad_low = lax.dynamic_slice_in_dim(cotangent, start, rows, 0)
     parts1, second, partial = feed_both(core_at, ffn_in1, grad_low, own1, other1)
-    second = lax.psum_scatter(second, "tensor", scatter_dimension=0, tiled=True)
-    second = lax.all_gather(
-        (hidden1 + second.astype(F32)).astype(BF), "tensor", axis=0, tiled=True
-    )
-    swapped = other_core(jnp.where(core == 0, second, passed))
-    section_output = in_core_order(core, jnp.where(core == 0, passed, second), swapped)
-
     def gain_sum(value, scale, grad):
         return jnp.sum(grad * value * scale, axis=0)
 
-    grad_ffn_in = scatter_sum(partial, "tensor")
-    keep1, send1 = feed_weights(core_at, ffn_in1, grad_low, parts1)
-    sum1 = (keep1.astype(F32) + other_core(send1)).astype(BF)
-    sum1 = sum1.reshape(-1, hidden_width)
+    sum1, done = feed_weights(ffn_in1, grad_low, parts1)
+    gain_rows = jnp.broadcast_to(gain_ffn[1][None], (8, width))
+    grad_hidden, copies, ffn_gain1 = back(
+        blocks_of(partial), shard_of(cotangent), hidden1, gain_rows, (done,)
+    )
+    ffn_gain1 = ffn_gain1[0]
+    sum1 = after(sum1.reshape(-1, hidden_width), grad_hidden)
     sum1 = lax.psum_scatter(sum1, DP, scatter_dimension=0, tiled=True)
-    ffn_gain1 = gain_sum(hidden1, scale_ffn1, grad_ffn_in)
-    grad_hidden = shard_of(cotangent) + rms_backward(hidden1, scale_ffn1, gain_ffn[1], grad_ffn_in)
-    hidden_low = gather(grad_hidden.astype(BF), "tensor")
+    hidden_low = gathered(copies)
     grad_output_t = dot_rows(hidden_low, attended).astype(BF)
     grad_attended = dot(hidden_low, output_t).astype(BF)
+    second = after(second, grad_attended)
+    second = (hidden1 + direct_scatter_sum(second, "tensor")).astype(BF)
     grad_query, grad_kv = whole(
         attend_backward_kernel,
         [jax.ShapeDtypeStruct((rows, 256), F32), jax.ShapeDtypeStruct((2 * rows, 256), F32)],
@@ -705,68 +979,44 @@
         vmem=20,
     )
     partial = dot_cols(grad_qkv, qkv_w)
-    mix_gain1 = jnp.sum(partial * passed.astype(F32) * scale_mix1, axis=0)
-    grad_normed = scatter_sum(partial.astype(BF), "tensor")
-    passed_f32 = passed_shard.astype(F32)
-    scale_shard = lax.dynamic_slice_in_dim(scale_mix1, lane * shard, shard, 0)
-    grad_passed = grad_hidden + rms_backward(passed_f32, scale_shard, gain_mix[1], grad_normed)
-    grad_shard = grad_passed.astype(BF)
-    grad_low = gather(grad_shard, "tensor")
+    grad_attn = jnp.concatenate([dot_rows(normed1, grad_qkv).astype(BF), grad_output_t], axis=1)
+    gain_rows = jnp.broadcast_to(gain_mix[1][None], (8, width))
+    grad_hidden, copies, mix_gain1 = back(
+        blocks_of(partial.astype(BF)), grad_hidden, passed_shard, gain_rows, (grad_attn,)
+    )
+    mix_gain1 = mix_gain1[0]
+    grad_shard = copies[0]
+    grad_low = gathered(copies)
     grad_passed = grad_low
 
-    parts0, partial = feed_backward(core_at, grad_low, own0, other0, acts0)
-    grad_ffn_in = scatter_sum(partial, "tensor")
-    keep0, send0 = feed_weights(core_at, ffn_in0, grad_low, parts0)
-    ffn_gain0 = gain_sum(hidden0, scale_ffn0, grad_ffn_in)
-    grad_hidden = grad_shard.astype(F32) + rms_backward(
-        hidden0, scale_ffn0, gain_ffn[0], grad_ffn_in
-    )
-
-    grad_attn = jnp.concatenate(
-        [dot_rows(normed1, grad_qkv).astype(BF), grad_output_t], axis=1
-    )
-
-    attn_sum = half_of(grad_attn, core).astype(F32) + other_core(half_of(grad_attn, 1 - core))
-    attn_sum = attn_sum.astype(BF).reshape(16, mix_rows, attn_cols)
-    attn_sum = jnp.pad(attn_sum, ((0, 0), (0, 0), (0, hidden_width - attn_cols)))
-    sum0 = (keep0.astype(F32) + other_core(send0)).astype(BF)
-    sum0 = jnp.concatenate([sum0, attn_sum], axis=1)
-    hidden_low = gather(grad_hidden.astype(BF), "tensor")
-    sum0 = after(sum0.reshape(-1, hidden_width), hidden_low)
+    parts0, partial = feed_backward(
+        core_at, grad_low, own0, other0, acts0, needs=(second,)
+    )
+    early = other_core(jnp.where(core == 0, grad_passed, passed))
+
+    sum0, done = feed_weights(ffn_in0, grad_low, parts0, (grad_attn,), (sum1,))
+    gain_rows = jnp.broadcast_to(gain_ffn[0][None], (8, width))
+    grad_hidden, copies, ffn_gain0 = back(
+        blocks_of(partial), grad_shard, hidden0, gain_rows, (done,)
+    )
+    ffn_gain0 = ffn_gain0[0]
+    hidden_low = gathered(copies)
+
+    sum0 = after(sum0.reshape(-1, hidden_width), grad_hidden)
     sum0 = lax.psum_scatter(sum0, DP, scatter_dimension=0, tiled=True)
-    grad_attn = sum0[3 * HALF :, :attn_cols].astype(F32)
-    sum0 = sum0[: 3 * HALF]
-    mine = jnp.where(core == 0, sum0, sum1).reshape(3, HALF, hidden_width)
-    theirs = other_core(jnp.where(core == 0, sum1, sum0)).reshape(3, HALF, hidden_width)
-    grad_gate, grad_up, grad_down = (
-        in_core_order(core, mine[k], theirs[k]).astype(F32) for k in range(3)
-    )
+    dense0 = sum0[: 3 * dp_rows]
+    theirs = other_core(jnp.where(core == 0, sum1, dense0)).astype(F32)
+    dense = jnp.where(core == 0, dense0, sum1).astype(F32) + theirs
+    grad_gate, grad_up, grad_down = (dense[k * dp_rows : (k + 1) * dp_rows] for k in range(3))
+    attn_both = sum0[3 * dp_rows :, :attn_cols]
+    grad_attn = half_of(attn_both, core).astype(F32) + other_core(half_of(attn_both, 1 - core))
 
     following = lax.ppermute(hidden_low[:HALO], "pipe", [(1, 0)])
-    hidden_more = jnp.concatenate([hidden_low, following], 0)
-    grad_out_t = dot_rows(hidden_low, convolved).astype(BF)
-    grad_convolved = dot(hidden_more, conv_out_t)
-    grad_out_gate = grad_convolved[:rows] * total
-    grad_total = grad_convolved * out_gate[HALO:]
-    grad_product = jnp.zeros((rows, channels), F32)
-    taps = []
-    for back in range(3):
-        mask = (near[HALO + back : HALO + back + rows] == near[HALO : HALO + rows])[:, None]
-        grad_product = grad_product + conv_kernel[2 - back] * jnp.where(
-            mask, grad_total[back : back + rows], 0.0
-        )
-        moved = product[HALO - back : HALO - back + rows]
-        taps.append(jnp.sum(jnp.where(same(back, rows), grad_total[:rows] * moved, 0.0), axis=0))
-    taps = jnp.stack(taps[::-1])
-    own = slice(HALO, HALO + rows)
-    grad_projected = jnp.concatenate(
-        [grad_product * signal[own], grad_out_gate, grad_product * in_gate[own]], axis=1
-    ).astype(BF)
-    grad_conv = jnp.concatenate(
-        [dot_rows(normed0[own], grad_projected).astype(BF), grad_out_t], axis=1
-    )
-    partial = dot_cols(grad_projected, conv_in_w)
-    mix_gain0 = jnp.sum(partial * window[own].astype(F32) * scale_mix0[own], axis=0)
+    grad_projected, partial, taps, mix_gain0 = conv_backward(
+        core_at, conv_half, conv_other, window, near, taps_in, projected, hidden_low, following,
+        needs=(early,),
+    )
+    taps, mix_gain0 = taps[:3], mix_gain0[0]
 
     taps_wide = lax.dynamic_update_slice_in_dim(
         jnp.zeros((3, width), F32), taps, lane * channels, 1
@@ -794,22 +1044,30 @@
         summed = jnp.sum(parts.astype(F32), axis=0)
         return summed[:-16], one_term(summed[-16:])
 
-    terms = exchange(jnp.broadcast_to(two_terms(small)[None], (4, 16, width)), "tensor")
-    small = one_term(jnp.sum(terms.astype(F32), axis=0))
+    grad_normed, small = sum_beside(partial.reshape(4, shard, width), small, "tensor")
     small = small + one_term(other_core(two_terms(small)).astype(F32))
-
-    grad_normed = direct_scatter_sum(partial.astype(BF), "tensor")
     tokens_shard = shard_of(tokens)
-    scale_shard = lax.dynamic_slice_in_dim(scale_mix0, HALO + lane * shard, shard, 0)
+    scale_shard = rms_forward(tokens_shard, gain_mix[0])[1]
     grad_tokens = grad_hidden + rms_backward(tokens_shard, scale_shard, gain_mix[0], grad_normed)
-    grad_tokens = direct_gather(grad_tokens.astype(BF), "tensor")
-    swapped = other_core(jnp.where(core == 0, grad_passed, grad_tokens))
-    input_grad = in_core_order(
-        core, jnp.where(core == 0, grad_tokens, grad_passed), swapped
+    late = jnp.concatenate([grad_tokens.astype(BF), second], axis=1)
+    keep, send = conv_weights(core_at, normed0, hidden_low, grad_projected, convolved)
+    blocks = keep.astype(F32) + other_core(send)
+    terms = jnp.broadcast_to(two_terms(small)[None], (16, 16, width))
+    blocks = jnp.concatenate([blocks.astype(BF).reshape(16, mix_rows, width), terms], 1)
+    grad_in, grad_out, small = last_sums(
+        exchange(blocks, DP), 3 * channels, ()
+    )
+
+    parts = [late, *(turned(late, "tensor", by) for by in (1, 3, 2))]
+    place = jnp.stack([lane, core]).astype(jnp.int32)
+    mine, send = arrange(place, parts, (small,))
+    swapped = other_core(send)
+    section_output = jnp.where(
+        core == 0, jnp.concatenate([passed, early], 0), jnp.concatenate([swapped, mine], 0)
+    )
+    input_grad = jnp.where(
+        core == 0, jnp.concatenate([mine, swapped], 0), jnp.concatenate([early, grad_passed], 0)
     ).astype(F32)
-
-    blocks = half_of(grad_conv, core).astype(F32) + other_core(half_of(grad_conv, 1 - core))
-    blocks, small = sum_beside(blocks.reshape(16, mix_rows, width), small, DP)
 
     def own_gain(pair):
         return lax.dynamic_slice(pair, (core, at_dp * dp_rows), (1, dp_rows))
@@ -822,9 +1080,9 @@
         grad_gate[None],
         grad_up[None],
         grad_down.T[None],
-        blocks[:, : 3 * channels].reshape(mix_rows, 3, channels),
+        grad_in.reshape(mix_rows, 3, channels),
         small[4:7],
-        blocks[:, 3 * channels :].T,
+        grad_out.T,
         grad_attn[:, :channels],
         grad_attn[:, channels : channels + 128],
         grad_attn[:, channels + 128 : 2 * channels],

time: 510 us -> 499 us (0.978)
  other arithmetic: 57.1 us -> 32.9 us
  Pallas kernels: 70.5 us -> 90.5 us
  blocking collectives: 100 us -> 82.5 us
  waiting for transfers between devices: 132 us -> 146 us
  matrix products: 16.2 us -> 5.95 us
  local copies, waits for them, and re-layouts: 32.5 us -> 41.7 us
    pallas_call x5 -> x13, Pallas kernels: 55 us -> 75.1 us  [the longest x3 35.3 us: feed(): pl.pallas_call(kernel, in_specs=in_specs + [ANY_SPEC] * len(needs), out_s...]
    all_to_all x5 -> x4, blocking collectives: 100 us -> 82.5 us  [exchange(): return lax.all_to_all(parts, axis, 0, 0)]
    unnamed x112 -> x126, local copies, waits for them, and re-layouts: 5.76 us -> 20.9 us
    all_to_all x10 -> x11, waiting for transfers between devices: 105 us -> 117 us  [exchange(): return lax.all_to_all(parts, axis, 0, 0)]
    dot_general x12 -> x6, matrix products: 16.2 us -> 5.95 us  [dot(): lax.dot_general(left, right, (dims, ((), ())), preferred_element_type=F32)]
    convert_element_type x12 -> x5, other arithmetic: 21.5 us -> 11.7 us  [the longest x1 5.11 us: per_device(): input_grad = jnp.where(core == 0, jnp.concatenate([mine, swapped], 0), jn...]
    ppermute x12 -> x10, starting transfers between devices: 16.4 us -> 12.7 us  [other_core(): return lax.ppermute(value, 'pipe', [(0, 1), (1, 0)])]
    all_to_all x10 -> x11, starting transfers between devices: 42 us -> 45.5 us  [exchange(): return lax.all_to_all(parts, axis, 0, 0)]
  transfers between devices with their start and end apart: 37 -> 34, of which waited for: 19 -> 19; matrix products, arithmetic and copies ran while one was open for 19% -> 11% of each run, Pallas kernels for 11% -> 15%
where the time goes in v1:
time: 499 us; the launch traced here: 489 us
  waiting for transfers between devices  146 us (29%)
  Pallas kernels  90.5 us (18%)
  blocking collectives  82.5 us (17%)
  starting transfers between devices  74.5 us (15%)
  local copies, waits for them, and re-layouts  41.7 us (8%)
  other arithmetic  32.9 us (7%)
  between operations  15.5 us (3%)
  matrix products  5.95 us (1%)
    all_to_all x11, waiting for transfers between devices, exchange(): return lax.all_to_all(parts, axis, 0, 0)  117 us
    all_to_all x4, blocking collectives, exchange(): return lax.all_to_all(parts, axis, 0, 0)  82.5 us
    all_to_all x11, starting transfers between devices, exchange(): return lax.all_to_all(parts, axis, 0, 0)  45.5 us
    pallas_call x3, Pallas kernels, feed(): pl.pallas_call(kernel, in_specs=in_specs + [ANY_SPEC] * len(needs), out_s...  35.3 us
    unnamed x126, local copies, waits for them, and re-layouts  20.9 us
    pallas_call x8, Pallas kernels, local(): pl.pallas_call(kernel, in_specs=in_specs + [ANY_SPEC] * len(needs), out_s...  20.3 us
    pallas_call x2, Pallas kernels, feed_weights(): pl.pallas_call(not_before(feed_weights_kernel, steps, len(needs)), grid=(...  19.5 us
    ppermute x6, waiting for transfers between devices, turned(): lax.ppermute(value, axis, [(i, (i + by) % size) for i in range(size)])  19.3 us
  transfers between devices with their start and end apart: 34, of which 19 were waited for; matrix products, arithmetic and copies ran while one was open for 11% of the time, Pallas kernels for 15%

profile of v1, /device:TPU:1, one launch (start us, length us, event | category | flops | bytes accessed | tf_op | source)
XLA Modules:
  0.0 489.1 jit_solution(16617286164553982025)
XLA Ops:
  14.9 29.7 %all_to_all.75.refs_1_ = bf16[16,40,1024]{2,1,0:T(8,128)(2,1)S(1)} all-to-all(bf16[16,40,1024]{2,1,0:T(8,128)(2,1)S(1)} %broadcast_in_dim.40), channel_id=1, replica_groups=mesh['pipe'=2,'tensor'=4,'dp_0'=4,'dp_1'=4] {'dp_0','dp_1'}, dimensions={0} | all-to-all | bytes 2621440 | tf_op jit(solution)/shard_map/all_to_all | solution.py:34
  44.6 2.6 collective-permute-start
  51.2 4.5 shard_map.288
  58.6 5.0 %all-to-all-start.1 = ((bf16[4,128,1024]{2,1,0:T(8,128)(2,1)}), bf16[4,128,1024]{2,1,0:T(8,128)(2,1)S(1)}, u32[]{:S(2)}, u32[]{:S(2)}) async-start(bf16[4,128,1024]{2,1,0:T(8,128)(2,1)} %bitcast.6), calls=%async_computation.1 | async-start | bytes 2097152 | tf_op jit(solution)/shard_map/all_to_all | solution.py:34
  63.7 14.5 %all-to-all-done.1 = bf16[4,128,1024]{2,1,0:T(8,128)(2,1)S(1)} async-done(((bf16[4,128,1024]{2,1,0:T(8,128)(2,1)}), bf16[4,128,1024]{2,1,0:T(8,128)(2,1)S(1)}, u32[]{:S(2)}, u32[]{:S(2)}) %all-to-all-start.1) | async-done | bytes 1048608 | tf_op jit(solution)/shard_map/all_to_all | solution.py:34
  81.4 18.1 %all_to_all.76 = bf16[4,128,1024]{2,1,0:T(8,128)(2,1)} all-to-all(bf16[4,128,1024]{2,1,0:T(8,128)(2,1)S(1)} %broadcast_in_dim.44), channel_id=1, replica_groups=mesh['pipe'=2,'tensor'=4,'dp_0'=4,'dp_1'=4] {'tensor'}, dimensions={0} | all-to-all | bytes 2097152 | tf_op jit(solution)/shard_map/all_to_all | solution.py:34
  99.5 9.1 %shard_map.289 = (f32[2,512,1152]{2,1,0:T(8,128)}, bf16[512,1024]{1,0:T(8,128)(2,1)}) custom-call(s32[1]{0:T(128)} %bitcast.refs_0_, bf16[512,1024]{1,0:T(8,128)(2,1)} %bitcast.102, bf16[16,128,1152]{2,1,0:T(8,128)(2,1)} %bitcast.97, bf16[16,128,1152]{2,1,0:T(8,128)(2,1)} %collective-permute-done.2.refs_3_), custom_call_target="tpu_custom_call" | custom-call | flops 3623878656 | bytes 16252932 | tf_op jit(solution)/shard_map/pallas_call | solution.py:444
  108.6 3.5 all-to-all-start.3
  112.7 13.4 %all-to-all-done.3 = bf16[4,128,1024]{2,1,0:T(8,128)(2,1)S(1)} async-done(((bf16[4,128,1024]{2,1,0:T(8,128)(2,1)}), bf16[4,128,1024]{2,1,0:T(8,128)(2,1)S(1)}, u32[]{:S(2)}, u32[]{:S(2)}) %all-to-all-start.3) | async-done | bytes 1048608 | tf_op jit(solution)/shard_map/all_to_all | solution.py:34
  128.2 3.7 all-to-all-start.4
  140.2 4.8 all-to-all-done.4
  151.0 3.9 collective-permute-done.3.refs_1_
  155.1 5.4 %shard_map.291 = (bf16[512,256]{1,0:T(8,128)(2,1)S(1)}, f32[8,512]{1,0:T(8,128)S(1)}) custom-call(bf16[512,512]{1,0:T(8,128)(2,1)S(1)} %shard_map.290.refs_0_, bf16[512,256]{1,0:T(8,128)(2,1)S(1)} %collective-permute-done.3.refs_1_, s32[1024,128]{1,0:T(8,128)S(1)} %broadcast_in_dim.47.refs_2_, s32[8,512]{1,0:T(8,128)S(1)} %broadcast_in_dim.48.refs_3_), custom_call_target="tpu_custom_call" | custom-call | flops 402653184 | bytes 1605632 | tf_op jit(solution)/shard_map/pallas_call | solution.py:140
  161.0 17.4 %all_to_all.77 = bf16[4,128,1024]{2,1,0:T(8,128)(2,1)S(1)} all-to-all(bf16[4,128,1024]{2,1,0:T(8,128)(2,1)S(1)} %bitcast.101), channel_id=1, replica_groups=mesh['pipe'=2,'tensor'=4,'dp_0'=4,'dp_1'=4] {'tensor'}, dimensions={0} | all-to-all | bytes 2097152 | tf_op jit(solution)/shard_map/all_to_all | solution.py:34
  181.3 4.7 all-to-all-start.6
  186.0 2.3 constant_dynamic-slice_fusion.4.refs_2_.refs_1_
  188.3 13.0 %all-to-all-done.6 = bf16[4,128,1024]{2,1,0:T(8,128)(2,1)} async-done(((bf16[4,128,1024]{2,1,0:T(8,128)(2,1)}), bf16[4,128,1024]{2,1,0:T(8,128)(2,1)}, u32[]{:S(2)}, u32[]{:S(2)}) %all-to-all-start.6) | async-done | bytes 1048608 | tf_op jit(solution)/shard_map/all_to_all | solution.py:34
  201.3 13.9 %shard_map.292 = (bf16[3,512,1152]{2,1,0:T(8,128)(2,1)}, bf16[512,1024]{1,0:T(8,128)(2,1)}, bf16[512,1024]{1,0:T(8,128)(2,1)}) custom-call(s32[1]{0:T(128)} %bitcast.refs_0_, bf16[512,1024]{1,0:T(8,128)(2,1)} %bitcast.31.refs_1_.refs_0_, bf16[512,1024]{1,0:T(8,128)(2,1)} %constant_dynamic-slice_fusion.4.refs_2_.refs_1_, bf16[16,96,1152]{2,1,0:T(8,128)(2,1)} %bitcast.138, ...), custom_call_target="tpu_custom_call" | custom-call | flops 7247757312 | bytes 14811140 | tf_op jit(solution)/shard_map/pallas_call | solution.py:444
  215.2 4.3 all-to-all-start.7
  221.3 9.1 %shard_map.293 = (bf16[16,192,1152]{2,1,0:T(8,128)(2,1)}, f32[8,128]{1,0:T(8,128)}) custom-call(bf16[512,1024]{1,0:T(8,128)(2,1)} %bitcast.31.refs_1_.refs_0_, bf16[512,1024]{1,0:T(8,128)(2,1)} %constant_dynamic-slice_fusion.4.refs_2_.refs_1_, bf16[3,512,1152]{2,1,0:T(8,128)(2,1)} %get-tuple-element.68.refs_2_), custom_call_target="tpu_custom_call" | custom-call | flops 1048576 | bytes 1048576 | tf_op jit(solution)/shard_map/pallas_call | solution.py:507
  230.5 3.4 all-to-all-done.7.refs_0_
  239.1 17.4 %all_to_all.78 = bf16[4,128,1024]{2,1,0:T(8,128)(2,1)S(1)} all-to-all(bf16[4,128,1024]{2,1,0:T(8,128)(2,1)} %copy-done.23), channel_id=1, replica_groups=mesh['pipe'=2,'tensor'=4,'dp_0'=4,'dp_1'=4] {'tensor'}, dimensions={0} | all-to-all | bytes 2097152 | tf_op jit(solution)/shard_map/all_to_all | solution.py:34
  257.5 6.1 %shard_map.295 = (f32[512,256]{1,0:T(8,128)S(1)}, f32[1024,256]{1,0:T(8,128)S(1)}) custom-call(bf16[512,512]{1,0:T(8,128)(2,1)S(1)} %copy-done.18, bf16[512,256]{1,0:T(8,128)(2,1)S(1)} %copy-done.39, s32[1024,128]{1,0:T(8,128)S(1)} %copy-done.29, s32[8,512]{1,0:T(8,128)S(1)} %broadcast_in_dim.48.refs_3_, f32[8,512]{1,0:T(8,128)S(1)} %get-tuple-element.64.refs_4_, ...), custom_call_target="tpu_custom_call" | custom-call | flops 1006632960 | bytes 3178496 | tf_op jit(solution)/shard_map/pallas_call | solution.py:140
  263.7 4.6 collective-permute-start.5
  273.4 4.2 all-to-all-start.9
  280.4 12.1 %all-to-all-done.9.refs_0_ = bf16[4,128,1024]{2,1,0:T(8,128)(2,1)} async-done(((bf16[4,128,1024]{2,1,0:T(8,128)(2,1)}), bf16[4,128,1024]{2,1,0:T(8,128)(2,1)}, u32[]{:S(2)}, u32[]{:S(2)}) %all-to-all-start.9) | async-done | bytes 1048608 | tf_op jit(solution)/shard_map/all_to_all | solution.py:34
  294.5 2.4 shard_map.297
  297.9 4.2 all-to-all-start.10
  308.0 13.4 %collective-permute-done.7 = bf16[128,1024]{1,0:T(8,128)(2,1)S(1)} collective-permute-done((bf16[128,1024]{1,0:T(8,128)(2,1)S(1)}, bf16[128,1024]{1,0:T(8,128)(2,1)S(1)}, u32[]{:S(2)}, u32[]{:S(2)}) %collective-permute-start.7) | collective-permute-done | bytes 262176 | tf_op jit(solution)/shard_map/ppermute | solution.py:59
  321.4 6.0 %collective-permute-done.9 = bf16[128,1024]{1,0:T(8,128)(2,1)S(1)} collective-permute-done((bf16[128,1024]{1,0:T(8,128)(2,1)S(1)}, bf16[128,1024]{1,0:T(8,128)(2,1)S(1)}, u32[]{:S(2)}, u32[]{:S(2)}) %collective-permute-start.9) | collective-permute-done | bytes 262176 | tf_op jit(solution)/shard_map/ppermute | solution.py:59
  329.3 12.2 %shard_map.298 = (bf16[3,512,1152]{2,1,0:T(8,128)(2,1)}, bf16[512,1024]{1,0:T(8,128)(2,1)}) custom-call(s32[1]{0:T(128)} %bitcast.refs_0_, bf16[512,1024]{1,0:T(8,128)(2,1)} %bitcast.36.refs_1_, bf16[16,128,1152]{2,1,0:T(8,128)(2,1)} %bitcast.99, bf16[16,128,1152]{2,1,0:T(8,128)(2,1)} %collective-permute-done.2.refs_3_, ...), custom_call_target="tpu_custom_call" | custom-call | flops 3623878656 | bytes 19791876 | tf_op jit(solution)/shard_map/pallas_call | solution.py:444
  341.6 3.5 all-to-all-start.11
  346.2 10.4 %shard_map.299 = (bf16[16,256,1152]{2,1,0:T(8,128)(2,1)}, f32[8,128]{1,0:T(8,128)}) custom-call(bf16[512,1024]{1,0:T(8,128)(2,1)} %bitcast.103, bf16[512,1024]{1,0:T(8,128)(2,1)} %bitcast.36.refs_1_, bf16[3,512,1152]{2,1,0:T(8,128)(2,1)} %get-tuple-element.80.refs_2_, bf16[1024,768]{1,0:T(8,128)(2,1)} %copy-done, ...), custom_call_target="tpu_custom_call" | custom-call | flops 1048576 | bytes 1048576 | tf_op jit(solution)/shard_map/pallas_call | solution.py:507
  360.9 2.7 bitcast_select_fusion
  363.7 3.1 collective-permute-start.6
  366.8 4.2 all-to-all-start.12
  371.0 15.3 %all-to-all-done.12 = bf16[4,128,1024]{2,1,0:T(8,128)(2,1)} async-done(((bf16[4,128,1024]{2,1,0:T(8,128)(2,1)}), bf16[4,128,1024]{2,1,0:T(8,128)(2,1)}, u32[]{:S(2)}, u32[]{:S(2)}) %all-to-all-start.12) | async-done | bytes 1048608 | tf_op jit(solution)/shard_map/all_to_all | solution.py:34
  387.1 2.9 collective-permute-start.10
  392.1 5.0 %shard_map.301 = (bf16[512,768]{1,0:T(8,128)(2,1)S(1)}, bf16[512,1024]{1,0:T(8,128)(2,1)S(1)}, f32[8,256]{1,0:T(8,128)S(1)}, f32[8,1024]{1,0:T(8,128)S(1)}) custom-call(s32[1]{0:T(128)} %bitcast.refs_0_, bf16[16,40,1024]{2,1,0:T(8,128)(2,1)S(1)} %all_to_all.75.refs_1_, bf16[16,40,1024]{2,1,0:T(8,128)(2,1)} %collective-permute-done.refs_2_, ...), custom_call_target="tpu_custom_call" | custom-call | flops 1073741824 | bytes 8929284 | tf_op jit(solution)/shard_map/pallas_call | solution.py:636
  399.1 2.5 pad_maximum_fusion.2
  401.6 4.3 all-to-all-start.13
  405.9 3.5 shard_map.302
  409.5 12.9 %all-to-all-done.13 = bf16[4,144,1024]{2,1,0:T(8,128)(2,1)} async-done(((bf16[4,144,1024]{2,1,0:T(8,128)(2,1)}), bf16[4,144,1024]{2,1,0:T(8,128)(2,1)}, u32[]{:S(2)}, u32[]{:S(2)}) %all-to-all-start.13) | async-done | bytes 1179680 | tf_op jit(solution)/shard_map/all_to_all | solution.py:34
  429.9 3.8 all-to-all-start.14
  436.6 2.4 collective-permute-start.12
  439.0 26.3 %all-to-all-done.14.refs_0_ = bf16[16,48,1024]{2,1,0:T(8,128)(2,1)S(1)} async-done(((bf16[16,48,1024]{2,1,0:T(8,128)(2,1)}), bf16[16,48,1024]{2,1,0:T(8,128)(2,1)S(1)}, u32[]{:S(2)}, u32[]{:S(2)}) %all-to-all-start.14) | async-done | bytes 1572896 | tf_op jit(solution)/shard_map/all_to_all | solution.py:34
  465.9 2.2 shard_map.304
  471.8 5.1 %fusion = (f32[1,1024,1024]{2,1,0:T(8,128)}, bf16[1,1024,1024]{2,1,0:T(8,128)(2,1)}) fusion(bf16[1,512,1024]{2,1,0:T(8,128)(2,1)S(1)} %bitcast.108, bf16[1,512,1024]{2,1,0:T(8,128)(2,1)S(1)} %bitcast.90, bf16[1,512,1024]{2,1,0:T(8,128)(2,1)} %bitcast.47, bf16[1,512,1024]{2,1,0:T(8,128)(2,1)} %bitcast.37, pred[]{:T(512)S(6)} %eq.2, ...), kind=kLoop, calls=%fused_computation.5 | loop fusion | flops 19922944 | bytes 11534337 | tf_op jit(solution)/shard_map/convert_element_type | solution.py:1070
  (309 shorter events, 94.5 us)
Async XLA Ops:
  7.2 72.3 %all-gather.5.cloned.1.call-start = ((), (), s32[]{:S(2)}) async-start(), calls=%async_computation.19 | async-start | bytes 5013504 | tf_op jit(solution)/shard_map/all_gather | solution.py:839
  10.4 2.6 collective-permute-start.1
  14.7 32.5 %copy-start.51 = (s32[1,1024]{1,0:T(1,128)S(1)}, s32[1,1024]{1,0:T(1,128)}, u32[]{:S(2)}) copy-start(s32[1,1024]{1,0:T(1,128)} %param.19) | copy-start | bytes 12292
  14.7 32.7 %copy-start.57 = (f32[3,256]{1,0:T(4,128)S(1)}, f32[3,256]{1,0:T(4,128)}, u32[]{:S(2)}) copy-start(f32[3,256]{1,0:T(4,128)} %param.26) | copy-start | bytes 9220
  44.6 5.4 %collective-permute-start = (bf16[16,40,1024]{2,1,0:T(8,128)(2,1)S(1)}, bf16[16,40,1024]{2,1,0:T(8,128)(2,1)}, u32[]{:S(2)}, u32[]{:S(2)}) collective-permute-start(bf16[16,40,1024]{2,1,0:T(8,128)(2,1)S(1)} %all_to_all.75.refs_1_), channel_id=1, source_target_pairs={{0,64},{64,0},{1,65},{65,1},{2,66},{66,2},{3,67},{67,3},{4,68},{68... | collective-permute-start | bytes 3932168 | tf_op jit(solution)/shard_map/ppermute | solution.py:89
  58.6 19.5 %all-to-all-start.1 = ((bf16[4,128,1024]{2,1,0:T(8,128)(2,1)}), bf16[4,128,1024]{2,1,0:T(8,128)(2,1)S(1)}, u32[]{:S(2)}, u32[]{:S(2)}) async-start(bf16[4,128,1024]{2,1,0:T(8,128)(2,1)} %bitcast.6), calls=%async_computation.1 | async-start | bytes 2097152 | tf_op jit(solution)/shard_map/all_to_all | solution.py:34
  63.6 115.1 %all-gather.7.cloned.1.call-start = ((), (), s32[]{:S(2)}) async-start(), calls=%async_computation.20 | async-start | bytes 3760128 | tf_op jit(solution)/shard_map/all_gather | solution.py:840
  79.5 20.0 %collective-permute-start.2 = (bf16[16,128,1152]{2,1,0:T(8,128)(2,1)}, bf16[16,128,1152]{2,1,0:T(8,128)(2,1)}, u32[]{:S(2)}, u32[]{:S(2)}) collective-permute-start(bf16[16,128,1152]{2,1,0:T(8,128)(2,1)} %bitcast.96), channel_id=1, source_target_pairs={{0,64},{64,0},{1,65},{65,1},{2,66},{66,2},{3,67},{67,3},{4,68},{68... | collective-permute-start | bytes 14155784 | tf_op jit(solution)/shard_map/ppermute | solution.py:89
  108.6 17.5 %all-to-all-start.3 = ((bf16[4,128,1024]{2,1,0:T(8,128)(2,1)}), bf16[4,128,1024]{2,1,0:T(8,128)(2,1)S(1)}, u32[]{:S(2)}, u32[]{:S(2)}) async-start(bf16[4,128,1024]{2,1,0:T(8,128)(2,1)} %bitcast.114), calls=%async_computation.3 | async-start | bytes 2097152 | tf_op jit(solution)/shard_map/all_to_all | solution.py:34
  128.2 16.8 %all-to-all-start.4 = ((bf16[4,128,1024]{2,1,0:T(8,128)(2,1)}), bf16[4,128,1024]{2,1,0:T(8,128)(2,1)S(1)}, u32[]{:S(2)}, u32[]{:S(2)}) async-start(bf16[4,128,1024]{2,1,0:T(8,128)(2,1)} %broadcast_in_dim.45), calls=%async_computation.4 | async-start | bytes 2097152 | tf_op jit(solution)/shard_map/all_to_all | solution.py:34
  149.6 5.2 %collective-permute-start.3 = (bf16[512,256]{1,0:T(8,128)(2,1)S(1)}, bf16[512,256]{1,0:T(8,128)(2,1)S(1)}, u32[]{:S(2)}, u32[]{:S(2)}) collective-permute-start(bf16[512,256]{1,0:T(8,128)(2,1)S(1)} %slice.179), channel_id=1, source_target_pairs={{0,64},{1,65},{2,66},{3,67},{4,68},{5,69},{6,70},{7,71},{8,72},{9,... | collective-permute-start | bytes 786440 | tf_op jit(solution)/shard_map/ppermute | solution.py:918
  154.9 23.5 %copy-start.38 = (bf16[512,256]{1,0:T(8,128)(2,1)}, bf16[512,256]{1,0:T(8,128)(2,1)S(1)}, u32[]{:S(2)}) copy-start(bf16[512,256]{1,0:T(8,128)(2,1)S(1)} %collective-permute-done.3.refs_1_) | copy-start | bytes 786436
  155.1 23.3 %copy-start.28 = (s32[1024,128]{1,0:T(8,128)}, s32[1024,128]{1,0:T(8,128)S(1)}, u32[]{:S(2)}) copy-start(s32[1024,128]{1,0:T(8,128)S(1)} %broadcast_in_dim.47.refs_2_) | copy-start | bytes 1572868
  160.5 18.1 %copy-start.32 = (bf16[512,256]{1,0:T(8,128)(2,1)}, bf16[512,256]{1,0:T(8,128)(2,1)S(1)}, u32[]{:S(2)}) copy-start(bf16[512,256]{1,0:T(8,128)(2,1)S(1)} %get-tuple-element.65) | copy-start | bytes 786436
  161.0 17.6 %copy-start.7 = (bf16[128,1024]{1,0:T(8,128)(2,1)S(1)}, bf16[128,1024]{1,0:T(8,128)(2,1)}, u32[]{:S(2)}) copy-start(bf16[128,1024]{1,0:T(8,128)(2,1)} %copy-done.6) | copy-start | bytes 786436
  178.7 55.1 %copy-start.3 = (f32[128,1024]{1,0:T(8,128)}, f32[128,1024]{1,0:T(8,128)S(1)}, u32[]{:S(2)}) copy-start(f32[128,1024]{1,0:T(8,128)S(1)} %get-tuple-element.164.refs_2_) | copy-start | bytes 1572868
  178.8 22.5 %collective-permute-start.4 = (bf16[16,96,1152]{2,1,0:T(8,128)(2,1)}, bf16[16,96,1152]{2,1,0:T(8,128)(2,1)}, u32[]{:S(2)}, u32[]{:S(2)}) collective-permute-start(bf16[16,96,1152]{2,1,0:T(8,128)(2,1)} %bitcast.137), channel_id=1, source_target_pairs={{0,64},{64,0},{1,65},{65,1},{2,66},{66,2},{3,67},{67,3},{4,68},{68... | collective-permute-start | bytes 10616840 | tf_op jit(solution)/shard_map/ppermute | solution.py:89
  181.3 20.0 %all-to-all-start.6 = ((bf16[4,128,1024]{2,1,0:T(8,128)(2,1)}), bf16[4,128,1024]{2,1,0:T(8,128)(2,1)}, u32[]{:S(2)}, u32[]{:S(2)}) async-start(bf16[4,128,1024]{2,1,0:T(8,128)(2,1)} %broadcast_in_dim.49), calls=%async_computation.6 | async-start | bytes 2097152 | tf_op jit(solution)/shard_map/all_to_all | solution.py:34
  215.2 18.7 %all-to-all-start.7 = ((bf16[4,128,1024]{2,1,0:T(8,128)(2,1)}), bf16[4,128,1024]{2,1,0:T(8,128)(2,1)}, u32[]{:S(2)}, u32[]{:S(2)}) async-start(bf16[4,128,1024]{2,1,0:T(8,128)(2,1)} %bitcast.112), calls=%async_computation.7 | async-start | bytes 2097152 | tf_op jit(solution)/shard_map/all_to_all | solution.py:34
  219.5 126.7 %reduce-scatter.3.cloned.1.call-start = ((), (), s32[]{:S(2)}) async-start(), calls=%async_computation.17 | async-start | bytes 7520256 | tf_op jit(solution)/shard_map/reduce_scatter | solution.py:949
  239.0 17.4 %copy-start.43 = (bf16[1024,768]{1,0:T(8,128)(2,1)S(1)}, bf16[1024,768]{1,0:T(8,128)(2,1)}, u32[]{:S(2)}) copy-start(bf16[1024,768]{1,0:T(8,128)(2,1)} %maximum_select_fusion.2) | copy-start | bytes 4718596
  239.1 18.4 %copy-start.18 = (bf16[512,512]{1,0:T(8,128)(2,1)S(1)}, bf16[512,512]{1,0:T(8,128)(2,1)}, u32[]{:S(2)}) copy-start(bf16[512,512]{1,0:T(8,128)(2,1)} %copy-done.17) | copy-start | bytes 1572868
  239.1 18.4 %copy-start.29 = (s32[1024,128]{1,0:T(8,128)S(1)}, s32[1024,128]{1,0:T(8,128)}, u32[]{:S(2)}) copy-start(s32[1024,128]{1,0:T(8,128)} %copy-done.28) | copy-start | bytes 1572868
  239.1 18.4 %copy-start.39 = (bf16[512,256]{1,0:T(8,128)(2,1)S(1)}, bf16[512,256]{1,0:T(8,128)(2,1)}, u32[]{:S(2)}) copy-start(bf16[512,256]{1,0:T(8,128)(2,1)} %copy-done.38) | copy-start | bytes 786436
  263.7 6.0 %collective-permute-start.5 = (f32[512,256]{1,0:T(8,128)S(1)}, f32[512,256]{1,0:T(8,128)S(1)}, u32[]{:S(2)}, u32[]{:S(2)}) collective-permute-start(f32[512,256]{1,0:T(8,128)S(1)} %get-tuple-element.172), channel_id=1, source_target_pairs={{64,0},{65,1},{66,2},{67,3},{68,4},{69,5},{70,6},{71,7},{72,8},{73... | collective-permute-start | bytes 1572872 | tf_op jit(solution)/shard_map/ppermute | solution.py:968
  273.4 19.1 %all-to-all-start.9 = ((bf16[4,128,1024]{2,1,0:T(8,128)(2,1)}), bf16[4,128,1024]{2,1,0:T(8,128)(2,1)}, u32[]{:S(2)}, u32[]{:S(2)}) async-start(bf16[4,128,1024]{2,1,0:T(8,128)(2,1)} %bitcast.113), calls=%async_computation.9 | async-start | bytes 2097152 | tf_op jit(solution)/shard_map/all_to_all | solution.py:34
  280.4 17.6 %copy-start = (bf16[1024,768]{1,0:T(8,128)(2,1)}, bf16[1024,768]{1,0:T(8,128)(2,1)S(1)}, u32[]{:S(2)}) copy-start(bf16[1024,768]{1,0:T(8,128)(2,1)S(1)} %pad_maximum_fusion.refs_4_.refs_3_) | copy-start | bytes 4718596
  297.9 31.4 %all-to-all-start.10 = ((bf16[4,128,1024]{2,1,0:T(8,128)(2,1)}), bf16[4,128,1024]{2,1,0:T(8,128)(2,1)}, u32[]{:S(2)}, u32[]{:S(2)}) async-start(bf16[4,128,1024]{2,1,0:T(8,128)(2,1)} %copy-done.16), calls=%async_computation.10 | async-start | bytes 2097152 | tf_op jit(solution)/shard_map/all_to_all | solution.py:34
  303.4 18.0 %collective-permute-start.7 = (bf16[128,1024]{1,0:T(8,128)(2,1)S(1)}, bf16[128,1024]{1,0:T(8,128)(2,1)S(1)}, u32[]{:S(2)}, u32[]{:S(2)}) collective-permute-start(bf16[128,1024]{1,0:T(8,128)(2,1)S(1)} %get-tuple-element.169), channel_id=1, source_target_pairs={{0,16},{16,32},{32,48},{48,0},{1,17},{17,33},{33,49},{49,1},{2,18}... | collective-permute-start | bytes 786440 | tf_op jit(solution)/shard_map/ppermute | solution.py:59
  304.8 16.5 %collective-permute-start.8 = (bf16[128,1024]{1,0:T(8,128)(2,1)S(1)}, bf16[128,1024]{1,0:T(8,128)(2,1)S(1)}, u32[]{:S(2)}, u32[]{:S(2)}) collective-permute-start(bf16[128,1024]{1,0:T(8,128)(2,1)S(1)} %get-tuple-element.171), channel_id=1, source_target_pairs={{0,48},{16,0},{32,16},{48,32},{1,49},{17,1},{33,17},{49,33},{2,50}... | collective-permute-start | bytes 786440 | tf_op jit(solution)/shard_map/ppermute | solution.py:59
  306.1 21.2 %collective-permute-start.9 = (bf16[128,1024]{1,0:T(8,128)(2,1)S(1)}, bf16[128,1024]{1,0:T(8,128)(2,1)S(1)}, u32[]{:S(2)}, u32[]{:S(2)}) collective-permute-start(bf16[128,1024]{1,0:T(8,128)(2,1)S(1)} %get-tuple-element.170), channel_id=1, source_target_pairs={{0,32},{16,48},{32,0},{48,16},{1,33},{17,49},{33,1},{49,17},{2,34}... | collective-permute-start | bytes 786440 | tf_op jit(solution)/shard_map/ppermute | solution.py:59
  341.6 16.5 %all-to-all-start.11 = ((bf16[4,128,1024]{2,1,0:T(8,128)(2,1)}), bf16[4,128,1024]{2,1,0:T(8,128)(2,1)S(1)}, u32[]{:S(2)}, u32[]{:S(2)}) async-start(bf16[4,128,1024]{2,1,0:T(8,128)(2,1)} %bitcast.111), calls=%async_computation.11 | async-start | bytes 2097152 | tf_op jit(solution)/shard_map/all_to_all | solution.py:34
  345.1 131.8 %reduce-scatter.5.cloned.1.call-start = ((), (), s32[]{:S(2)}) async-start(), calls=%async_computation.18 | async-start | bytes 10027008 | tf_op jit(solution)/shard_map/reduce_scatter | solution.py:1006
  360.9 29.7 %copy-start.2 = (bf16[544,1024]{1,0:T(8,128)(2,1)S(1)}, bf16[544,1024]{1,0:T(8,128)(2,1)}, u32[]{:S(2)}) copy-start(bf16[544,1024]{1,0:T(8,128)(2,1)} %copy-done.1) | copy-start | bytes 3342340
  360.9 29.7 %copy-start.5 = (s32[544,256]{1,0:T(8,128)S(1)}, s32[544,256]{1,0:T(8,128)}, u32[]{:S(2)}) copy-start(s32[544,256]{1,0:T(8,128)} %copy-done.4) | copy-start | bytes 1671172
  363.7 26.5 %collective-permute-start.6 = (bf16[512,1024]{1,0:T(8,128)(2,1)}, bf16[512,1024]{1,0:T(8,128)(2,1)}, u32[]{:S(2)}, u32[]{:S(2)}) collective-permute-start(bf16[512,1024]{1,0:T(8,128)(2,1)} %bitcast_select_fusion), channel_id=1, source_target_pairs={{0,64},{64,0},{1,65},{65,1},{2,66},{66,2},{3,67},{67,3},{4,68},{68... | collective-permute-start | bytes 3145736 | tf_op jit(solution)/shard_map/ppermute | solution.py:89
  366.8 19.6 %all-to-all-start.12 = ((bf16[4,128,1024]{2,1,0:T(8,128)(2,1)}), bf16[4,128,1024]{2,1,0:T(8,128)(2,1)}, u32[]{:S(2)}, u32[]{:S(2)}) async-start(bf16[4,128,1024]{2,1,0:T(8,128)(2,1)} %copy-done.21), calls=%async_computation.13 | async-start | bytes 2097152 | tf_op jit(solution)/shard_map/all_to_all | solution.py:34
  387.1 3.5 collective-permute-start.10
  401.6 20.8 %all-to-all-start.13 = ((bf16[4,144,1024]{2,1,0:T(8,128)(2,1)}), bf16[4,144,1024]{2,1,0:T(8,128)(2,1)}, u32[]{:S(2)}, u32[]{:S(2)}) async-start(bf16[4,144,1024]{2,1,0:T(8,128)(2,1)} %pad_maximum_fusion.2), calls=%async_computation.14 | async-start | bytes 2359296 | tf_op jit(solution)/shard_map/all_to_all | solution.py:34
  409.4 16.6 %collective-permute-start.14 = (bf16[512,1024]{1,0:T(8,128)(2,1)}, bf16[512,1024]{1,0:T(8,128)(2,1)S(1)}, u32[]{:S(2)}, u32[]{:S(2)}) collective-permute-start(bf16[512,1024]{1,0:T(8,128)(2,1)} %get-tuple-element.98), channel_id=1, source_target_pairs={{0,64},{64,0},{1,65},{65,1},{2,66},{66,2},{3,67},{67,3},{4,68},{68... | collective-permute-start | bytes 3145736 | tf_op jit(solution)/shard_map/ppermute | solution.py:89
  424.0 1.9 collective-permute-start.15
  429.9 35.4 %all-to-all-start.14 = ((bf16[16,48,1024]{2,1,0:T(8,128)(2,1)}), bf16[16,48,1024]{2,1,0:T(8,128)(2,1)S(1)}, u32[]{:S(2)}, u32[]{:S(2)}) async-start(bf16[16,48,1024]{2,1,0:T(8,128)(2,1)} %pad_maximum_fusion.1), calls=%async_computation.15 | async-start | bytes 3145728 | tf_op jit(solution)/shard_map/all_to_all | solution.py:34
  436.2 29.8 %collective-permute-start.11 = (bf16[128,2048]{1,0:T(8,128)(2,1)S(1)}, bf16[128,2048]{1,0:T(8,128)(2,1)S(1)}, u32[]{:S(2)}, u32[]{:S(2)}) collective-permute-start(bf16[128,2048]{1,0:T(8,128)(2,1)S(1)} %pad_maximum_fusion.3.refs_1_), channel_id=1, source_target_pairs={{0,16},{16,32},{32,48},{48,0},{1,17},{17,33},{33,49},{49,1},{2,18}... | collective-permute-start | bytes 1572872 | tf_op jit(solution)/shard_map/ppermute | solution.py:59
  436.6 29.4 %collective-permute-start.12 = (bf16[128,2048]{1,0:T(8,128)(2,1)S(1)}, bf16[128,2048]{1,0:T(8,128)(2,1)S(1)}, u32[]{:S(2)}, u32[]{:S(2)}) collective-permute-start(bf16[128,2048]{1,0:T(8,128)(2,1)S(1)} %pad_maximum_fusion.3.refs_1_), channel_id=1, source_target_pairs={{0,48},{16,0},{32,16},{48,32},{1,49},{17,1},{33,17},{49,33},{2,50}... | collective-permute-start | bytes 1572872 | tf_op jit(solution)/shard_map/ppermute | solution.py:59
  438.9 27.0 %collective-permute-start.13 = (bf16[128,2048]{1,0:T(8,128)(2,1)S(1)}, bf16[128,2048]{1,0:T(8,128)(2,1)}, u32[]{:S(2)}, u32[]{:S(2)}) collective-permute-start(bf16[128,2048]{1,0:T(8,128)(2,1)S(1)} %pad_maximum_fusion.3.refs_1_), channel_id=1, source_target_pairs={{0,32},{16,48},{32,0},{48,16},{1,33},{17,49},{33,1},{49,17},{2,34}... | collective-permute-start | bytes 1572872 | tf_op jit(solution)/shard_map/ppermute | solution.py:59
  468.1 3.7 collective-permute-start.16
  477.9 1.7 collective-permute-start.18
  479.1 2.0 collective-permute-start.17
  (48 other events, 189.5 us)
Sparse Core Ops, SparseCore 0:
  14.7 62.0 all-gather.4
  81.2 46.1 all-gather.6
  239.2 77.9 reduce-scatter.2
  361.0 98.8 reduce-scatter.4
